TPU v7x, 32 devices: a whole 2x2x4 slice. The times are simulated.
32 devices in a mesh: scene: 2 (over x), gx: 16 (over z, y, core).
Axes of the slice: x: 2, y: 2, z: 4, core: 2. Of those that a mesh axis runs over, the one named last changes fastest.
Arguments:
- voxels: bfloat16 [64, 128, 8, 128], P(('scene', 'gx')), parts along dimension 0, may hold values from -6 to 6
- prior: float32 [64, 128, 8], P(('scene', 'gx')), parts along dimension 0, may hold values from -6 to 410
- conv_first: bfloat16 [27, 128, 128], replicated, may hold values from -0.109375 to 0.109375
- conv_second: bfloat16 [27, 128, 128], replicated, may hold values from -0.109375 to 0.109375
- score_x: bfloat16 [128, 128], replicated, may hold values from -2 to 2
- score_y: bfloat16 [128, 128], replicated, may hold values from -1.5 to 1.5
- plane_yz_w: bfloat16 [9, 128, 128], replicated, may hold values from -0.1875 to 0.1875
- plane_xz_w: bfloat16 [9, 128, 128], replicated, may hold values from -0.1875 to 0.1875
- norm_gain: float32 [128], replicated, may hold values from 0.1 to 1.9
- mlp_in: bfloat16 [128, 512], replicated, may hold values from -0.5 to 0.5
- mlp_out: bfloat16 [512, 128], replicated, may hold values from -0.25 to 0.25
Outputs:
- encoded: bfloat16 [64, 128, 8, 128], P(('scene', 'gx')), parts along dimension 0
There are 2 independent parts, one for each index of `scene`. A program takes and returns all parts, laid end to end along the dimension named above; an argument that names none is the same for every part. Nothing has to cross between parts.
All inputs are finite; a program needn't handle non-finite values.
Results may differ from a plain program's by a relative error of at most 0.012.
Values may be sent and summed in bfloat16 or wider, within the bound.
A program may use at most 64 MiB of HBM per device.

v0:
```python
import jax
import jax.numpy as jnp
from jax import lax
from jax.sharding import PartitionSpec as P


def padded_2(shard, sides, width):
    for axis, dim in sides:
        devices, length = (lax.axis_size(axis), shard.shape[dim])
        up = [(i, (i + 1) % devices) for i in range(devices - 1)]
        down = [(j, i) for i, j in up]
        last = lax.slice_in_dim(shard, length - width, length, axis=dim)
        first = lax.slice_in_dim(shard, 0, width, axis=dim)
        before = lax.ppermute(last, axis, up)
        after = lax.ppermute(first, axis, down)
        shard = jnp.concatenate([before, shard, after], axis=dim)
    return shard


def activate(values):
    return jax.nn.gelu(values, approximate=True)


def stack_depth(field):
    depth = field.shape[-2]
    widths = [(0, 0)] * (field.ndim - 2) + [(1, 1), (0, 0)]
    padded = jnp.pad(field, widths)
    return jnp.concatenate([padded[..., shift : shift + depth, :] for shift in range(3)], axis=-1)


def volume_conv(extended, weight):
    rows = extended.shape[0] - 2
    across = extended.shape[1]
    depth = extended.shape[2]
    channels = weight.shape[-1]
    stacked = stack_depth(jnp.pad(extended, ((0, 0), (1, 1), (0, 0), (0, 0))))
    kernel = weight.reshape(3, 3, 3 * channels, channels)
    total = None
    for along_x in range(3):
        for along_y in range(3):
            window = stacked[along_x : along_x + rows, along_y : along_y + across].reshape(
                -1, 3 * channels
            )
            term = jnp.dot(window, kernel[along_x, along_y], preferred_element_type=jnp.float32)
            total = term if total is None else total + term
    return total.reshape(rows, across, depth, channels)


def plane_conv(extended, weight):
    rows = extended.shape[0] - 2
    depth = extended.shape[1]
    channels = weight.shape[-1]
    stacked = stack_depth(extended)
    kernel = weight.reshape(3, 3 * channels, channels)
    total = None
    for along in range(3):
        window = stacked[along : along + rows].reshape(-1, 3 * channels)
        term = jnp.dot(window, kernel[along], preferred_element_type=jnp.float32)
        total = term if total is None else total + term
    return total.reshape(rows, depth, channels)


def with_faces(field):
    return padded_2(field, (("gx", 0),), 1)


def replicated_plane(norm_sum, weighted, weight):
    pooled = (weighted / norm_sum).astype(jnp.bfloat16)
    extended = jnp.pad(pooled, ((1, 1), (0, 0), (0, 0)))
    return plane_conv(extended, weight).astype(jnp.bfloat16)


def on_device(
    voxels,
    prior,
    conv_first,
    conv_second,
    score_x,
    score_y,
    plane_yz_w,
    plane_xz_w,
    norm_gain,
    mlp_in,
    mlp_out,
):
    rows, across, depth, channels = voxels.shape
    first = activate(volume_conv(with_faces(voxels), conv_first)).astype(jnp.bfloat16)
    feature_in = with_faces(first)
    feature = (volume_conv(feature_in, conv_second) + voxels.astype(jnp.float32)).astype(
        jnp.bfloat16
    )
    flat = feature.reshape(-1, channels)
    logit_x = (
        jnp.dot(flat, score_x, preferred_element_type=jnp.float32).reshape(voxels.shape)
        + prior[..., None]
    )
    logit_y = (
        jnp.dot(flat, score_y, preferred_element_type=jnp.float32).reshape(voxels.shape)
        + prior[..., None]
    )
    feature_f = feature.astype(jnp.float32)
    pooled_xz = jnp.sum(jax.nn.softmax(logit_y, axis=1) * feature_f, axis=1).astype(jnp.bfloat16)
    strip = padded_2(pooled_xz, (("gx", 0),), 1)
    plane_xz = plane_conv(strip, plane_xz_w).astype(jnp.bfloat16)
    local_peak = jnp.max(logit_x, axis=0)
    peak = lax.pmax(local_peak.astype(jnp.bfloat16), "gx").astype(local_peak.dtype)
    weights = jnp.exp(logit_x - peak)
    norm_sum, weighted = lax.psum(
        (jnp.sum(weights, axis=0), jnp.sum(weights * feature_f, axis=0)), "gx"
    )
    plane_yz = replicated_plane(norm_sum, weighted, plane_yz_w)
    mixing = plane_yz.astype(jnp.float32)[None] + plane_xz.astype(jnp.float32)[:, None]
    joined = feature_f * mixing
    scale = lax.rsqrt(jnp.mean(joined * joined, axis=-1, keepdims=True) + 1e-06)
    normed = (joined * scale * norm_gain).astype(jnp.bfloat16)
    hidden = activate(
        jnp.dot(normed.reshape(-1, channels), mlp_in, preferred_element_type=jnp.float32)
    ).astype(jnp.bfloat16)
    update = jnp.dot(hidden, mlp_out, preferred_element_type=jnp.float32).reshape(voxels.shape)
    return (joined + update).astype(jnp.bfloat16)


def solution(mesh):
    return jax.shard_map(
        on_device,
        mesh=mesh,
        in_specs=(
            P(("scene", "gx"), None, None, None),
            P(("scene", "gx"), None, None),
            P(),
            P(),
            P(),
            P(),
            P(),
            P(),
            P(),
            P(),
            P(),
        ),
        out_specs=P(("scene", "gx"), None, None, None),
        check_vma=False,
    )
```

profile of v0, /device:TPU:0, one launch (start us, length us, event | category | flops | bytes accessed | tf_op | source)
XLA Modules:
  0.0 259.1 jit_solution(5800322310936605871)
XLA Ops:
  6.5 1.1 fusion.73
  7.6 2.4 collective-permute-start
  10.0 1.3 collective-permute-start.1
  11.3 4.2 %collective-permute-done.1 = bf16[1,128,8,128]{3,2,1,0:T(8,128)(2,1)S(1)} collective-permute-done((bf16[1,128,8,128]{3,2,1,0:T(8,128)(2,1)S(1)}, bf16[1,128,8,128]{3,2,1,0:T(8,128)(2,1)S(1)}, u32[]{:S(2)}, u32[]{:S(2)}) %collective-permute-start.1) | collective-permute-done | bytes 262176 | tf_op jit(solution)/shard_map/ppermute | solution.py:15
  15.6 1.1 fusion.25
  17.2 0.6 pad_maximum_fusion
  17.8 1.8 fusion.70
  25.2 6.7 %collective-permute-start.2 = (bf16[1,128,8,128]{3,2,1,0:T(8,128)(2,1)S(1)}, bf16[1,128,8,128]{3,2,1,0:T(8,128)(2,1)S(1)}, u32[]{:S(2)}, u32[]{:S(2)}) collective-permute-start(bf16[1,128,8,128]{3,2,1,0:T(8,128)(2,1)S(1)} %get-tuple-element.34), channel_id=1, source_target_pairs={{0,1},{1,2},{2,3},{3,4},{4,5},{5,6},{6,7},{7,8},{8,9},{9,10},{10,1... | collective-permute-start | bytes 786440 | tf_op jit(solution)/shard_map/ppermute | solution.py:14
  31.9 1.5 collective-permute-start.3
  33.5 1.9 collective-permute-done.3
  36.4 1.8 fusion.69
  44.2 0.6 fusion.78
  44.9 7.0 %collective-permute-start.4 = (bf16[1,8,128]{2,1,0:T(8,128)(2,1)S(1)}, bf16[1,8,128]{2,1,0:T(8,128)(2,1)S(1)}, u32[]{:S(2)}, u32[]{:S(2)}) collective-permute-start(bf16[1,8,128]{2,1,0:T(8,128)(2,1)S(1)} %get-tuple-element.48), channel_id=1, source_target_pairs={{0,1},{1,2},{2,3},{3,4},{4,5},{5,6},{6,7},{7,8},{8,9},{9,10},{10,1... | collective-permute-start | bytes 6152 | tf_op jit(solution)/shard_map/ppermute | solution.py:14
  51.8 1.3 collective-permute-start.5
  53.1 1.1 fusion.81
  54.9 91.3 %all-reduce.11.cloned.1.call-done = bf16[128,8,128]{2,0,1:T(8,128)(2,1)} async-done(((bf16[128,8,128]{2,0,1:T(8,128)(2,1)}), bf16[128,8,128]{2,0,1:T(8,128)(2,1)}) %all-reduce.11.cloned.1.call-update) | async-done | bytes 262160 | tf_op jit(solution)/shard_map/pmax | solution.py:106
  146.2 1.0 convert_element_type.86
  147.2 1.3 fusion.37
  148.9 95.0 %all-reduce.13.cloned.1.call-done = (f32[128,8,128]{2,0,1:T(8,128)}, f32[128,8,128]{2,0,1:T(8,128)}) async-done(((f32[128,8,128]{2,0,1:T(8,128)}, f32[128,8,128]{2,0,1:T(8,128)}), (f32[128,8,128]{2,0,1:T(8,128)}, f32[128,8,128]{2,0,1:T(8,128)})) %all-reduce.13.cloned.1.call-update) | async-done | bytes 1048592 | tf_op jit(solution)/shard_map/psum | solution.py:108
  244.0 1.3 divide_convert_fusion
  246.6 0.6 convolution_add_fusion.19
  247.2 0.6 fusion.17
  249.1 1.7 fusion.11
  251.1 1.1 copy.36
  (75 shorter events, 17.0 us)
Async XLA Ops:
  6.5 242.5 %copy-start = (bf16[512,128]{1,0:T(8,128)(2,1)S(1)}, bf16[512,128]{1,0:T(8,128)(2,1)}, u32[]{:S(2)}) copy-start(bf16[512,128]{1,0:T(8,128)(2,1)} %param.21) | copy-start | bytes 393220
  6.5 139.7 %all-reduce.11.cloned.1.call-start = ((), (), s32[]{:S(2)}) async-start(), calls=%async_computation | async-start | bytes 524288 | tf_op jit(solution)/shard_map/pmax | solution.py:106
  7.6 3.7 %collective-permute-start = (bf16[1,128,8,128]{3,2,1,0:T(8,128)(2,1)S(1)}, bf16[1,128,8,128]{3,2,1,0:T(8,128)(2,1)S(1)}, u32[]{:S(2)}, u32[]{:S(2)}) collective-permute-start(bf16[1,128,8,128]{3,2,1,0:T(8,128)(2,1)S(1)} %get-tuple-element.36), channel_id=1, source_target_pairs={{0,1},{1,2},{2,3},{3,4},{4,5},{5,6},{6,7},{7,8},{8,9},{9,10},{10,1... | collective-permute-start | bytes 786440 | tf_op jit(solution)/shard_map/ppermute | solution.py:14
  10.0 5.5 %collective-permute-start.1 = (bf16[1,128,8,128]{3,2,1,0:T(8,128)(2,1)S(1)}, bf16[1,128,8,128]{3,2,1,0:T(8,128)(2,1)S(1)}, u32[]{:S(2)}, u32[]{:S(2)}) collective-permute-start(bf16[1,128,8,128]{3,2,1,0:T(8,128)(2,1)S(1)} %get-tuple-element.37), channel_id=1, source_target_pairs={{1,0},{2,1},{3,2},{4,3},{5,4},{6,5},{7,6},{8,7},{9,8},{10,9},{11,1... | collective-permute-start | bytes 786440 | tf_op jit(solution)/shard_map/ppermute | solution.py:15
  17.8 1.8 copy-start.2
  24.8 8.6 %copy-start.4 = (bf16[9,128,128]{2,1,0:T(8,128)(2,1)S(1)}, bf16[9,128,128]{2,1,0:T(8,128)(2,1)}, u32[]{:S(2)}) copy-start(bf16[9,128,128]{2,1,0:T(8,128)(2,1)} %param.17) | copy-start | bytes 884740
  24.8 8.6 %copy-start.5 = (bf16[9,128,128]{2,1,0:T(8,128)(2,1)S(1)}, bf16[9,128,128]{2,1,0:T(8,128)(2,1)}, u32[]{:S(2)}) copy-start(bf16[9,128,128]{2,1,0:T(8,128)(2,1)} %param.18) | copy-start | bytes 884740
  25.2 8.3 %collective-permute-start.2 = (bf16[1,128,8,128]{3,2,1,0:T(8,128)(2,1)S(1)}, bf16[1,128,8,128]{3,2,1,0:T(8,128)(2,1)S(1)}, u32[]{:S(2)}, u32[]{:S(2)}) collective-permute-start(bf16[1,128,8,128]{3,2,1,0:T(8,128)(2,1)S(1)} %get-tuple-element.34), channel_id=1, source_target_pairs={{0,1},{1,2},{2,3},{3,4},{4,5},{5,6},{6,7},{7,8},{8,9},{9,10},{10,1... | collective-permute-start | bytes 786440 | tf_op jit(solution)/shard_map/ppermute | solution.py:14
  31.9 3.4 %collective-permute-start.3 = (bf16[1,128,8,128]{3,2,1,0:T(8,128)(2,1)S(1)}, bf16[1,128,8,128]{3,2,1,0:T(8,128)(2,1)S(1)}, u32[]{:S(2)}, u32[]{:S(2)}) collective-permute-start(bf16[1,128,8,128]{3,2,1,0:T(8,128)(2,1)S(1)} %get-tuple-element.35), channel_id=1, source_target_pairs={{1,0},{2,1},{3,2},{4,3},{5,4},{6,5},{7,6},{8,7},{9,8},{10,9},{11,1... | collective-permute-start | bytes 786440 | tf_op jit(solution)/shard_map/ppermute | solution.py:15
  36.3 1.8 copy-start.3
  42.8 1.0 copy-start.1
  43.4 0.7 copy-start.7
  43.4 0.8 copy-start.10
  44.2 8.9 %copy-start.6 = (bf16[128,128]{1,0:T(8,128)(2,1)S(1)}, bf16[128,128]{1,0:T(8,128)(2,1)}, u32[]{:S(2)}) copy-start(bf16[128,128]{1,0:T(8,128)(2,1)} %param.15) | copy-start | bytes 98308
  44.9 9.6 %collective-permute-start.4 = (bf16[1,8,128]{2,1,0:T(8,128)(2,1)S(1)}, bf16[1,8,128]{2,1,0:T(8,128)(2,1)S(1)}, u32[]{:S(2)}, u32[]{:S(2)}) collective-permute-start(bf16[1,8,128]{2,1,0:T(8,128)(2,1)S(1)} %get-tuple-element.48), channel_id=1, source_target_pairs={{0,1},{1,2},{2,3},{3,4},{4,5},{5,6},{6,7},{7,8},{8,9},{9,10},{10,1... | collective-permute-start | bytes 6152 | tf_op jit(solution)/shard_map/ppermute | solution.py:14
  51.8 3.1 %collective-permute-start.5 = (bf16[1,8,128]{2,1,0:T(8,128)(2,1)S(1)}, bf16[1,8,128]{2,1,0:T(8,128)(2,1)S(1)}, u32[]{:S(2)}, u32[]{:S(2)}) collective-permute-start(bf16[1,8,128]{2,1,0:T(8,128)(2,1)S(1)} %get-tuple-element.49), channel_id=1, source_target_pairs={{1,0},{2,1},{3,2},{4,3},{5,4},{6,5},{7,6},{8,7},{9,8},{10,9},{11,1... | collective-permute-start | bytes 6152 | tf_op jit(solution)/shard_map/ppermute | solution.py:15
  54.2 189.7 %all-reduce.13.cloned.1.call-start = ((), (), s32[]{:S(2)}) async-start(), calls=%async_computation.1 | async-start | bytes 2097152 | tf_op jit(solution)/shard_map/psum | solution.py:108
  247.2 1.1 copy-start.8
  248.2 0.9 copy-start.9
Sparse Core Ops, SparseCore 0:
  54.3 91.8 all-reduce.10
  150.2 93.7 all-reduce.12
where the time goes:
time: 260 us; the launch traced here: 259 us
  waiting for transfers between devices  193 us (74%)
  starting transfers between devices  20.3 us (8%)
  matrix products  15.8 us (6%)
  between operations  13.9 us (5%)
  local copies, waits for them, and re-layouts  8.71 us (3%)
  other arithmetic  7.42 us (3%)
    psum x1, waiting for transfers between devices, on_device(): lax.psum((jnp.sum(weights, axis=0), jnp.sum(weights * feature_f, axis=0))...  95 us
    pmax x1, waiting for transfers between devices, on_device(): lax.pmax(local_peak.astype(jnp.bfloat16), 'gx').astype(local_peak.dtype)  91.3 us
    ppermute x3, starting transfers between devices, padded_2(): before = lax.ppermute(last, axis, up)  16 us
    dot_general x18, matrix products, volume_conv(): jnp.dot(window, kernel[along_x, along_y], preferred_element_type=jnp.floa...  10.3 us
    ppermute x3, waiting for transfers between devices, padded_2(): after = lax.ppermute(first, axis, down)  6.46 us
  transfers between devices with their start and end apart: 8, of which 5 were waited for; matrix products, arithmetic and copies ran while one was open for 1% of the time, Pallas kernels for 0%

commit v1 on v0

v1 whole, which is shorter than its diff:
```python
import functools

import jax
import jax.numpy as jnp
from jax import lax
from jax.experimental import pallas as pl
from jax.experimental.pallas import tpu as pltpu
from jax.sharding import PartitionSpec as P

MESH = pl.DeviceIdType.MESH
PAD = 16
F32 = jnp.float32
BF16 = jnp.bfloat16


def activate(values):
    return jax.nn.gelu(values, approximate=True)


def stages_of(length, devices):
    stages, distance = [], 1
    while distance < devices:
        halves = length // 2 >= 16 and (length // 2) % 16 == 0
        length = length // 2 if halves else length
        stages.append((distance, length, halves))
        distance *= 2
    return stages


def shifted(values, depth):
    rows = values.shape[0]
    at_z = lax.broadcasted_iota(jnp.int32, values.shape, 0) % depth
    below = jnp.where(at_z == 0, 0.0, pltpu.roll(values, 1, 0))
    above = jnp.where(at_z == depth - 1, 0.0, pltpu.roll(values, rows - 1, 0))
    return below, values, above


def neighbourhood(padded, start, tile, depth):
    window = padded[pl.ds(pl.multiple_of(start, 16), tile + 2 * PAD), :].astype(F32)
    parts = shifted(window, depth)
    columns = []
    for along in (-1, 0, 1):
        first = PAD + along * depth
        for part in parts:
            columns.append(part[first : first + tile].astype(BF16))
    return jnp.concatenate(columns, axis=1)


def dot(a, b):
    return jnp.dot(a, b, preferred_element_type=F32)


def kernel(
    n,
    tile,
    stages,
    voxels,
    prior,
    conv_first,
    conv_second,
    score_x,
    score_y,
    plane_yz_w,
    plane_xz_w,
    norm_gain,
    mlp_in,
    mlp_out,
    out,
    w_first,
    w_second,
    w_score,
    w_yz,
    w_xz,
    w_in,
    w_out,
    vox,
    face_vox,
    first,
    face_first,
    acc,
    feature,
    stats,
    pooled,
    strip,
    halves,
    load_sem,
    vox_sem,
    face_send,
    face_recv,
    strip_send,
    strip_recv,
    rs_send,
    rs_recv,
    ag_send,
    ag_recv,
):
    me = lax.axis_index("gx")
    length, channels = voxels.shape[1], voxels.shape[2]
    depth = prior.shape[2]
    tiles = length // tile
    has_left, has_right = me > 0, me < n - 1
    left, right = me - 1, me + 1
    bits = [(me // distance) % 2 for distance, _, _ in stages]
    partners = [me + (1 - 2 * bit) * stage[0] for bit, stage in zip(bits, stages)]

    loads = [
        (conv_first.at[tap], w_first.at[:, pl.ds((2 - tap) * channels, channels)]) for tap in range(3)
    ]
    loads += [
        (conv_second.at[tap], w_second.at[:, pl.ds((2 - tap) * channels, channels)])
        for tap in range(3)
    ]
    loads += [
        (score_x, w_score.at[:, pl.ds(0, channels)]),
        (score_y, w_score.at[:, pl.ds(channels, channels)]),
        (plane_yz_w, w_yz),
        (plane_xz_w, w_xz),
        (mlp_in, w_in),
        (mlp_out, w_out),
    ]
    vox_loads = [
        pltpu.make_async_copy(
            voxels.at[row], vox.at[row, pl.ds(PAD, length), :], vox_sem.at[row]
        )
        for row in range(2)
    ]
    loads = [
        pltpu.make_async_copy(source, target, load_sem.at[i])
        for i, (source, target) in enumerate(loads)
    ]
    for copy in vox_loads + loads:
        copy.start()

    barrier = pltpu.get_barrier_semaphore()
    for partner in partners:
        pl.semaphore_signal(barrier, inc=1, device_id={"gx": partner}, device_id_type=MESH)

    @pl.when(has_left)
    def _():
        pl.semaphore_signal(barrier, inc=1, device_id={"gx": left}, device_id_type=MESH)

    @pl.when(has_right)
    def _():
        pl.semaphore_signal(barrier, inc=1, device_id={"gx": right}, device_id_type=MESH)

    edge = jnp.zeros((2, PAD, channels), BF16)
    for padded in (vox, face_vox, first, face_first):
        padded[:, 0:PAD, :] = edge
        padded[:, PAD + length :, :] = edge
    pooled[0:PAD, :] = edge[0]
    pooled[PAD + length :, :] = edge[0]

    for side, has in ((0, has_left), (1, has_right)):

        @pl.when(jnp.logical_not(has))
        def _():
            blank = jnp.zeros((length, channels), BF16)
            face_vox[side, pl.ds(PAD, length), :] = blank
            face_first[side, pl.ds(PAD, length), :] = blank
            strip[3 * side] = jnp.zeros(strip.shape[1:], F32)

    pl.semaphore_wait(barrier, len(stages) + jnp.where(has_left, 1, 0) + jnp.where(has_right, 1, 0))

    def face_copy(which, source, target, side, t, to):
        return pltpu.make_async_remote_copy(
            src_ref=source,
            dst_ref=target.at[1 - side, pl.ds(pl.multiple_of(PAD + t * tile, 16), tile), :],
            send_sem=face_send.at[which, side, t],
            recv_sem=face_recv.at[which, 1 - side, t],
            device_id={"gx": to},
            device_id_type=MESH,
        )

    def vox_copy(side, t):
        source = voxels.at[side, pl.ds(pl.multiple_of(t * tile, 16), tile), :]
        return face_copy(0, source, face_vox, side, t, (left, right)[side])

    def first_copy(side, t):
        source = first.at[side, pl.ds(pl.multiple_of(PAD + t * tile, 16), tile), :]
        return face_copy(1, source, face_first, side, t, (left, right)[side])

    def arrive(make, side, t, has):
        @pl.when(has)
        def _():
            make(1 - side, t).wait_recv()

    def sent(make):
        for side, has in ((0, has_left), (1, has_right)):

            @pl.when(has)
            def _():
                for t in range(tiles):
                    make(side, t).wait_send()

    for t in range(tiles):
        for side, has in ((0, has_left), (1, has_right)):

            @pl.when(has)
            def _():
                vox_copy(side, t).start()

    def inner(source, weight):
        def body(t, _):
            start = t * tile
            total = dot(neighbourhood(source.at[0], start, tile, depth), weight[:, channels:])
            total += dot(
                neighbourhood(source.at[1], start, tile, depth), weight[:, : 2 * channels]
            )
            acc[pl.ds(pl.multiple_of(start, 16), tile), :] = total
            return 0

        lax.fori_loop(0, tiles, body, 0)

    def outer(face, make, weight, side, t):
        has = (has_left, has_right)[side]
        if isinstance(t, int) and t == 0:
            arrive(make, side, 0, has)
        if t + 1 < tiles:
            arrive(make, side, t + 1, has)
        start = t * tile
        low = 2 * channels * (1 - side)
        return acc[start : start + tile, side * channels : (side + 1) * channels] + dot(
            neighbourhood(face.at[side], start, tile, depth), weight[:, low : low + channels]
        )

    for copy in vox_loads + loads[:3]:
        copy.wait()
    inner(vox, w_first)
    for t in range(tiles):
        for side, has in ((0, has_left), (1, has_right)):
            value = activate(outer(face_vox, vox_copy, w_first, side, t)).astype(BF16)
            first[side, PAD + t * tile : PAD + (t + 1) * tile, :] = value

            @pl.when(has)
            def _():
                first_copy(side, t).start()

    for copy in loads[3:]:
        copy.wait()
    inner(first, w_second)

    cells = tile // depth
    eye = lax.broadcasted_iota(jnp.int32, (cells, depth, depth), 1) == lax.broadcasted_iota(
        jnp.int32, (cells, depth, depth), 2
    )
    running = [None, None]
    for t in range(tiles):
        logits, features = [], []
        for side in range(2):
            start = PAD + t * tile
            value = outer(face_first, first_copy, w_second, side, t)
            value += vox[side, start : start + tile, :].astype(F32)
            value = value.astype(BF16)
            feature[side, t * tile : (t + 1) * tile, :] = value
            both = dot(value, w_score[...])
            field = prior[side, t * cells : (t + 1) * cells, :]
            field = jnp.broadcast_to(field[:, None, :], (cells, depth, depth))
            field = jnp.sum(jnp.where(eye, field, 0.0), axis=2, keepdims=True)
            field = jnp.broadcast_to(field, (cells, depth, channels))
            value = value.astype(F32)
            logits.append(both[:, :channels] + field.reshape(tile, channels))
            features.append(value)
            logit_y = both[:, channels:].reshape(cells, depth, channels) + field
            value = value.reshape(cells, depth, channels)
            peak = jnp.max(logit_y, axis=0)
            if running[side] is None:
                weight = jnp.exp(logit_y - peak[None])
                running[side] = (peak, jnp.sum(weight, 0), jnp.sum(weight * value, 0))
            else:
                old, norm, total = running[side]
                peak = jnp.maximum(peak, old)
                weight = jnp.exp(logit_y - peak[None])
                keep = jnp.exp(old - peak)
                running[side] = (
                    peak,
                    norm * keep + jnp.sum(weight, 0),
                    total * keep + jnp.sum(weight * value, 0),
                )
        peak = jnp.maximum(logits[0], logits[1]).astype(BF16)
        weights = [jnp.exp(logit - peak.astype(F32)) for logit in logits]
        at = slice(t * tile, (t + 1) * tile)
        stats[0, at, :] = peak
        stats[1, at, :] = (weights[0] + weights[1]).astype(BF16)
        stats[2, at, :] = (weights[0] * features[0] + weights[1] * features[1]).astype(BF16)

    def reduce_copy(k, start):
        rows = stages[k][1]
        return pltpu.make_async_remote_copy(
            src_ref=stats.at[:, pl.ds(pl.multiple_of(start, 16), rows), :],
            dst_ref=halves[k],
            send_sem=rs_send.at[k],
            recv_sem=rs_recv.at[k],
            device_id={"gx": partners[k]},
            device_id_type=MESH,
        )

    for side in range(2):
        _, norm, total = running[side]
        strip[1 + side] = (total / norm).astype(BF16).astype(F32)

    def strip_copy(side):
        return pltpu.make_async_remote_copy(
            src_ref=strip.at[1 + side],
            dst_ref=strip.at[3 - 3 * side],
            send_sem=strip_send.at[side],
            recv_sem=strip_recv.at[1 - side],
            device_id={"gx": (left, right)[side]},
            device_id_type=MESH,
        )

    start = 0
    pending = []
    for k, (distance, rows, halved) in enumerate(stages):
        if halved:
            give, keep = start + (1 - bits[k]) * rows, start + bits[k] * rows
        else:
            give = keep = start
        copy = reduce_copy(k, give)
        copy.start()
        pending.append(copy)
        if k == 0:
            for side, has in ((0, has_left), (1, has_right)):

                @pl.when(has)
                def _():
                    strip_copy(side).start()

        copy.wait_recv()
        if not halved:
            copy.wait_send()
            pending.pop()
        start = pl.multiple_of(keep, 16)
        mine = stats[:, pl.ds(start, rows), :].astype(F32)
        other = halves[k][...].astype(F32)
        peak = jnp.maximum(mine[0], other[0])
        up, down = jnp.exp(mine[0] - peak), jnp.exp(other[0] - peak)
        norm = mine[1] * up + other[1] * down
        total = mine[2] * up + other[2] * down
        if k + 1 < len(stages):
            stats[:, pl.ds(start, rows), :] = jnp.stack([peak, norm, total]).astype(BF16)
        else:
            pooled[pl.ds(pl.multiple_of(PAD + start, 16), rows), :] = (total / norm).astype(BF16)

    for k, (distance, rows, halved) in reversed(list(enumerate(stages))):
        if not halved:
            continue
        part = pooled.at[pl.ds(pl.multiple_of(PAD + start, 16), rows), :]
        copy = pltpu.make_async_remote_copy(
            src_ref=part,
            dst_ref=part,
            send_sem=ag_send.at[k],
            recv_sem=ag_recv.at[k],
            device_id={"gx": partners[k]},
            device_id_type=MESH,
        )
        copy.start()
        pending.append(copy)
        copy.wait_recv()
        start = start - bits[k] * rows

    for side, has in ((0, has_left), (1, has_right)):

        @pl.when(has)
        def _():
            strip_copy(1 - side).wait_recv()

    rows_z = [shifted(strip[i], depth) for i in range(4)]
    stacked = [
        jnp.concatenate([part for i in range(3) for part in rows_z[x + i]], axis=1)
        for x in range(2)
    ]
    plane_xz = dot(jnp.concatenate(stacked, axis=0).astype(BF16), w_xz[...])
    plane_xz = plane_xz.astype(BF16).astype(F32)
    gain = norm_gain[...]

    def finish(t, _):
        at = pl.ds(pl.multiple_of(t * tile, 16), tile)
        plane_yz = dot(neighbourhood(pooled, t * tile, tile, depth), w_yz[...])
        plane_yz = plane_yz.astype(BF16).astype(F32).reshape(cells, depth, channels)
        for side in range(2):
            mixing = plane_yz + plane_xz[side * depth : (side + 1) * depth][None]
            joined = feature[side, at, :].astype(F32) * mixing.reshape(tile, channels)
            scale = lax.rsqrt(jnp.mean(joined * joined, axis=-1, keepdims=True) + 1e-06)
            normed = (joined * scale * gain).astype(BF16)
            hidden = activate(dot(normed, w_in[...])).astype(BF16)
            out[side, at, :] = (joined + dot(hidden, w_out[...])).astype(BF16)
        return 0

    lax.fori_loop(0, tiles, finish, 0)

    for copy in pending:
        copy.wait_send()
    sent(vox_copy)
    sent(first_copy)
    for side, has in ((0, has_left), (1, has_right)):

        @pl.when(has)
        def _():
            strip_copy(side).wait_send()


def on_device(
    n,
    voxels,
    prior,
    conv_first,
    conv_second,
    score_x,
    score_y,
    plane_yz_w,
    plane_xz_w,
    norm_gain,
    mlp_in,
    mlp_out,
):
    rows, across, depth, channels = voxels.shape
    assert rows == 2 and depth == 8 and n & (n - 1) == 0
    length = across * depth
    hidden = mlp_in.shape[1]
    tile = min(256, length)
    tiles = length // tile
    stages = stages_of(length, n)
    padded = length + 2 * PAD
    taps = conv_first.shape[0] // 3 * channels
    hbm = pl.BlockSpec(memory_space=pl.ANY)
    vmem = pl.BlockSpec(memory_space=pltpu.VMEM)
    result = pl.pallas_call(
        functools.partial(kernel, n, tile, stages),
        out_shape=jax.ShapeDtypeStruct((rows, length, channels), BF16),
        in_specs=[hbm, vmem, hbm, hbm, hbm, hbm, hbm, hbm, vmem, hbm, hbm],
        out_specs=vmem,
        scratch_shapes=[
            pltpu.VMEM((taps, 3 * channels), BF16),
            pltpu.VMEM((taps, 3 * channels), BF16),
            pltpu.VMEM((channels, 2 * channels), BF16),
            pltpu.VMEM((taps, channels), BF16),
            pltpu.VMEM((taps, channels), BF16),
            pltpu.VMEM((channels, hidden), BF16),
            pltpu.VMEM((hidden, channels), BF16),
            pltpu.VMEM((2, padded, channels), BF16),
            pltpu.VMEM((2, padded, channels), BF16),
            pltpu.VMEM((2, padded, channels), BF16),
            pltpu.VMEM((2, padded, channels), BF16),
            pltpu.VMEM((length, 2 * channels), F32),
            pltpu.VMEM((2, length, channels), BF16),
            pltpu.VMEM((3, length, channels), BF16),
            pltpu.VMEM((padded, channels), BF16),
            pltpu.VMEM((4, depth, channels), F32),
            [pltpu.VMEM((3, stage[1], channels), BF16) for stage in stages],
            pltpu.SemaphoreType.DMA((12,)),
            pltpu.SemaphoreType.DMA((2,)),
            pltpu.SemaphoreType.DMA((2, 2, tiles)),
            pltpu.SemaphoreType.DMA((2, 2, tiles)),
            pltpu.SemaphoreType.DMA((2,)),
            pltpu.SemaphoreType.DMA((2,)),
            pltpu.SemaphoreType.DMA((len(stages),)),
            pltpu.SemaphoreType.DMA((len(stages),)),
            pltpu.SemaphoreType.DMA((len(stages),)),
            pltpu.SemaphoreType.DMA((len(stages),)),
        ],
        compiler_params=pltpu.CompilerParams(
            collective_id=0, has_side_effects=True, vmem_limit_bytes=48 * 1024 * 1024
        ),
    )(
        voxels.reshape(rows, length, channels),
        prior,
        conv_first.reshape(3, taps, channels),
        conv_second.reshape(3, taps, channels),
        score_x,
        score_y,
        plane_yz_w.reshape(taps, channels),
        plane_xz_w.reshape(taps, channels),
        norm_gain.reshape(1, channels),
        mlp_in,
        mlp_out,
    )
    return result.reshape(voxels.shape)


def solution(mesh):
    split = P(("scene", "gx"), None, None, None)
    return jax.shard_map(
        functools.partial(on_device, mesh.shape["gx"]),
        mesh=mesh,
        in_specs=(split, P(("scene", "gx"), None, None)) + (P(),) * 9,
        out_specs=split,
        check_vma=False,
    )
```

time: 260 us -> 60.3 us (0.23)
  the two profiles are of different devices: /device:TPU:0 before, /device:TPU:17 now
where the time goes in v1:
time: 60.3 us; the launch traced here: 59.9 us
  Pallas kernels  50.4 us (84%)
  local copies, waits for them, and re-layouts  9.42 us (16%)
    pallas_call x1, Pallas kernels, on_device(): pl.pallas_call(functools.partial(kernel, n, tile, stages), out_shape=jax....  50.4 us
    unnamed x22, local copies, waits for them, and re-layouts  9.42 us

profile of v1, /device:TPU:17, one launch (start us, length us, event | category | flops | bytes accessed | tf_op | source)
XLA Modules:
  0.0 59.9 jit_solution(558423073293796785)
XLA Ops:
  0.0 0.0 copy-start.5
  0.0 0.0 copy-start.9
  0.0 0.9 %copy.12.prior = f32[2,128,8]{2,1,0:T(8,128)S(1)} copy(f32[2,128,8]{1,2,0:T(8,128)} %param.12) | data formatting | bytes 16384 | tf_op args[1]
  0.9 0.1 copy-done.5
  0.9 0.0 copy-done.9
  0.9 0.0 copy-start
  0.9 1.2 %copy-done = bf16[27,128,128]{2,1,0:T(8,128)(2,1)S(1)} copy-done((bf16[27,128,128]{2,1,0:T(8,128)(2,1)S(1)}, bf16[27,128,128]{2,1,0:T(8,128)(2,1)}, u32[]{:S(2)}) %copy-start) | copy-done | bytes 884760
  2.1 0.0 copy-start.1
  2.1 1.2 %copy-done.1 = bf16[27,128,128]{2,1,0:T(8,128)(2,1)S(1)} copy-done((bf16[27,128,128]{2,1,0:T(8,128)(2,1)S(1)}, bf16[27,128,128]{2,1,0:T(8,128)(2,1)}, u32[]{:S(2)}) %copy-start.1) | copy-done | bytes 884760
  3.3 0.0 copy-start.2
  3.3 1.0 %copy-done.2 = bf16[2,128,8,128]{3,2,1,0:T(8,128)(2,1)S(1)} copy-done((bf16[2,128,8,128]{3,2,1,0:T(8,128)(2,1)S(1)}, bf16[2,128,8,128]{3,2,1,0:T(8,128)(2,1)}, u32[]{:S(2)}) %copy-start.2) | copy-done | bytes 524312
  4.3 0.0 copy-start.3
  4.3 1.0 %copy-done.3 = bf16[9,128,128]{2,1,0:T(8,128)(2,1)S(1)} copy-done((bf16[9,128,128]{2,1,0:T(8,128)(2,1)S(1)}, bf16[9,128,128]{2,1,0:T(8,128)(2,1)}, u32[]{:S(2)}) %copy-start.3) | copy-done | bytes 294936
  5.3 0.0 copy-start.4
  5.3 1.0 %copy-done.4 = bf16[9,128,128]{2,1,0:T(8,128)(2,1)S(1)} copy-done((bf16[9,128,128]{2,1,0:T(8,128)(2,1)S(1)}, bf16[9,128,128]{2,1,0:T(8,128)(2,1)}, u32[]{:S(2)}) %copy-start.4) | copy-done | bytes 294936
  6.2 0.0 copy-start.6
  6.2 0.9 %copy-done.6 = bf16[512,128]{1,0:T(8,128)(2,1)S(1)} copy-done((bf16[512,128]{1,0:T(8,128)(2,1)S(1)}, bf16[512,128]{1,0:T(8,128)(2,1)}, u32[]{:S(2)}) %copy-start.6) | copy-done | bytes 131096
  7.1 0.0 copy-start.7
  7.1 0.8 %copy-done.7 = bf16[128,128]{1,0:T(8,128)(2,1)S(1)} copy-done((bf16[128,128]{1,0:T(8,128)(2,1)S(1)}, bf16[128,128]{1,0:T(8,128)(2,1)}, u32[]{:S(2)}) %copy-start.7) | copy-done | bytes 32792
  7.9 0.0 copy-start.8
  7.9 0.8 %copy-done.8 = bf16[128,128]{1,0:T(8,128)(2,1)S(1)} copy-done((bf16[128,128]{1,0:T(8,128)(2,1)S(1)}, bf16[128,128]{1,0:T(8,128)(2,1)}, u32[]{:S(2)}) %copy-start.8) | copy-done | bytes 32792
  8.6 50.4 %shard_map.109 = bf16[2,1024,128]{2,1,0:T(8,128)(2,1)S(1)} custom-call(bf16[2,1024,128]{2,1,0:T(8,128)(2,1)S(1)} %bitcast.10, f32[2,128,8]{2,1,0:T(8,128)S(1)} %copy.12.prior, bf16[3,1152,128]{2,1,0:T(8,128)(2,1)S(1)} %bitcast.8, bf16[3,1152,128]{2,1,0:T(8,128)(2,1)S(1)} %bitcast.9, bf16[128,128]{1,0:T(8,128)(2,1)S(1)} %copy-done.7, ...), custom_call_target="tpu_custom_call" | custom-call | tf_op jit(solution)/shard_map/pallas_call | solution.py:427
  59.1 0.8 %copy.14 = bf16[2,128,8,128]{3,2,1,0:T(8,128)(2,1)} copy(bf16[2,128,8,128]{3,2,1,0:T(8,128)(2,1)S(1)} %bitcast.7) | data formatting | bytes 1048576
Async XLA Ops:
  0.0 0.9 %copy-start.5 = (bf16[128,512]{1,0:T(8,128)(2,1)S(1)}, bf16[128,512]{1,0:T(8,128)(2,1)}, u32[]{:S(2)}) copy-start(bf16[128,512]{1,0:T(8,128)(2,1)} %mlp_in.1) | copy-start | bytes 393220
  0.0 0.9 %copy-start.9 = (f32[128]{0:T(128)S(1)}, f32[128]{0:T(128)}, u32[]{:S(2)}) copy-start(f32[128]{0:T(128)} %param.19) | copy-start | bytes 1540
  0.9 1.2 %copy-start = (bf16[27,128,128]{2,1,0:T(8,128)(2,1)S(1)}, bf16[27,128,128]{2,1,0:T(8,128)(2,1)}, u32[]{:S(2)}) copy-start(bf16[27,128,128]{2,1,0:T(8,128)(2,1)} %param.13) | copy-start | bytes 2654212
  2.1 1.2 %copy-start.1 = (bf16[27,128,128]{2,1,0:T(8,128)(2,1)S(1)}, bf16[27,128,128]{2,1,0:T(8,128)(2,1)}, u32[]{:S(2)}) copy-start(bf16[27,128,128]{2,1,0:T(8,128)(2,1)} %param.14) | copy-start | bytes 2654212
  3.3 1.0 %copy-start.2 = (bf16[2,128,8,128]{3,2,1,0:T(8,128)(2,1)S(1)}, bf16[2,128,8,128]{3,2,1,0:T(8,128)(2,1)}, u32[]{:S(2)}) copy-start(bf16[2,128,8,128]{3,2,1,0:T(8,128)(2,1)} %param.11) | copy-start | bytes 1572868
  4.3 1.0 %copy-start.3 = (bf16[9,128,128]{2,1,0:T(8,128)(2,1)S(1)}, bf16[9,128,128]{2,1,0:T(8,128)(2,1)}, u32[]{:S(2)}) copy-start(bf16[9,128,128]{2,1,0:T(8,128)(2,1)} %param.17) | copy-start | bytes 884740
  5.3 1.0 %copy-start.4 = (bf16[9,128,128]{2,1,0:T(8,128)(2,1)S(1)}, bf16[9,128,128]{2,1,0:T(8,128)(2,1)}, u32[]{:S(2)}) copy-start(bf16[9,128,128]{2,1,0:T(8,128)(2,1)} %param.18) | copy-start | bytes 884740
  6.2 0.9 %copy-start.6 = (bf16[512,128]{1,0:T(8,128)(2,1)S(1)}, bf16[512,128]{1,0:T(8,128)(2,1)}, u32[]{:S(2)}) copy-start(bf16[512,128]{1,0:T(8,128)(2,1)} %mlp_out.1) | copy-start | bytes 393220
  7.1 0.8 %copy-start.7 = (bf16[128,128]{1,0:T(8,128)(2,1)S(1)}, bf16[128,128]{1,0:T(8,128)(2,1)}, u32[]{:S(2)}) copy-start(bf16[128,128]{1,0:T(8,128)(2,1)} %score_x.1) | copy-start | bytes 98308
  7.9 0.8 %copy-start.8 = (bf16[128,128]{1,0:T(8,128)(2,1)S(1)}, bf16[128,128]{1,0:T(8,128)(2,1)}, u32[]{:S(2)}) copy-start(bf16[128,128]{1,0:T(8,128)(2,1)} %score_y.1) | copy-start | bytes 98308

commit v2 on v1

--- a/solution.py
+++ b/solution.py
@@ -17,14 +17,25 @@
     return jax.nn.gelu(values, approximate=True)
 
 
-def stages_of(length, devices):
-    stages, distance = [], 1
-    while distance < devices:
-        halves = length // 2 >= 16 and (length // 2) % 16 == 0
-        length = length // 2 if halves else length
-        stages.append((distance, length, halves))
-        distance *= 2
+def stages_of(rows, devices):
+    count = devices.bit_length() - 1
+    bits = [[i] for i in range(min(2, count))]
+    bits += [list(range(i, min(i + 2, count))) for i in range(2, count, 2)]
+    stages = []
+    for group in bits:
+        radix = 1 << len(group)
+        shares = rows % (16 * radix) == 0
+        rows = rows // radix if shares else rows
+        stages.append((1 << group[0], radix, rows, shares))
     return stages
+
+
+def far_radix(stages):
+    total = 1
+    for distance, radix, _, shares in stages:
+        if shares and distance > 1:
+            total *= radix
+    return total
 
 
 def shifted(values, depth):
@@ -96,12 +107,31 @@
 ):
     me = lax.axis_index("gx")
     length, channels = voxels.shape[1], voxels.shape[2]
-    depth = prior.shape[2]
+    depth = prior.shape[1]
     tiles = length // tile
     has_left, has_right = me > 0, me < n - 1
     left, right = me - 1, me + 1
-    bits = [(me // distance) % 2 for distance, _, _ in stages]
-    partners = [me + (1 - 2 * bit) * stage[0] for bit, stage in zip(bits, stages)]
+    across = length // depth
+
+    def across_bits(distance, hop):
+        other, weight = me, 1
+        while weight <= hop:
+            bit = (me // (distance * weight)) % 2
+            if hop & weight:
+                other = other + (1 - 2 * bit) * distance * weight
+            weight *= 2
+        return other
+
+    digits = [(me // distance) % radix for distance, radix, _, _ in stages]
+    partners = []
+    for distance, radix, _, _ in stages:
+        found = {}
+        for hop in range(1, radix):
+            other = across_bits(distance, hop)
+            found[hop] = (other, (other // distance) % radix)
+        partners.append(found)
+    slots = [sum(stage[1] - 1 for stage in stages[:k]) for k in range(len(stages))]
+    far = [across_bits(2, hop) for hop in range(1, far_radix(stages))]
 
     loads = [
         (conv_first.at[tap], w_first.at[:, pl.ds((2 - tap) * channels, channels)]) for tap in range(3)
@@ -132,7 +162,13 @@
         copy.start()
 
     barrier = pltpu.get_barrier_semaphore()
-    for partner in partners:
+    greeted = far + [
+        partner
+        for stage, found in zip(stages, partners)
+        for partner, _ in found.values()
+        if stage[0] == 1 or not stage[3]
+    ]
+    for partner in greeted:
         pl.semaphore_signal(barrier, inc=1, device_id={"gx": partner}, device_id_type=MESH)
 
     @pl.when(has_left)
@@ -159,7 +195,7 @@
             face_first[side, pl.ds(PAD, length), :] = blank
             strip[3 * side] = jnp.zeros(strip.shape[1:], F32)
 
-    pl.semaphore_wait(barrier, len(stages) + jnp.where(has_left, 1, 0) + jnp.where(has_right, 1, 0))
+    pl.semaphore_wait(barrier, len(greeted) + jnp.where(has_left, 1, 0) + jnp.where(has_right, 1, 0))
 
     def face_copy(which, source, target, side, t, to):
         return pltpu.make_async_remote_copy(
@@ -240,11 +276,12 @@
     inner(first, w_second)
 
     cells = tile // depth
-    eye = lax.broadcasted_iota(jnp.int32, (cells, depth, depth), 1) == lax.broadcasted_iota(
-        jnp.int32, (cells, depth, depth), 2
-    )
+    cube = (cells, depth, across)
+    lane = lax.broadcasted_iota(jnp.int32, cube, 2)
+    cell = lax.broadcasted_iota(jnp.int32, cube, 0)
     running = [None, None]
-    for t in range(tiles):
+
+    def local_part(t):
         logits, features = [], []
         for side in range(2):
             start = PAD + t * tile
@@ -253,9 +290,9 @@
             value = value.astype(BF16)
             feature[side, t * tile : (t + 1) * tile, :] = value
             both = dot(value, w_score[...])
-            field = prior[side, t * cells : (t + 1) * cells, :]
-            field = jnp.broadcast_to(field[:, None, :], (cells, depth, depth))
-            field = jnp.sum(jnp.where(eye, field, 0.0), axis=2, keepdims=True)
+            field = jnp.broadcast_to(prior[side][None], cube)
+            field = jnp.where(lane == cell + t * cells, field, 0.0)
+            field = jnp.sum(field, axis=2, keepdims=True)
             field = jnp.broadcast_to(field, (cells, depth, channels))
             value = value.astype(F32)
             logits.append(both[:, :channels] + field.reshape(tile, channels))
@@ -283,20 +320,85 @@
         stats[1, at, :] = (weights[0] + weights[1]).astype(BF16)
         stats[2, at, :] = (weights[0] * features[0] + weights[1] * features[1]).astype(BF16)
 
-    def reduce_copy(k, start):
-        rows = stages[k][1]
-        return pltpu.make_async_remote_copy(
-            src_ref=stats.at[:, pl.ds(pl.multiple_of(start, 16), rows), :],
-            dst_ref=halves[k],
-            send_sem=rs_send.at[k],
-            recv_sem=rs_recv.at[k],
-            device_id={"gx": partners[k]},
+    def rows_at(start, rows):
+        return pl.ds(pl.multiple_of(start, 16), rows)
+
+    starts = [t * tile for t in range(tiles)]
+    pending = []
+    flying = {}
+
+    def reduce_start(g, k):
+        distance, radix, rows, shares = stages[k]
+        mine = digits[k]
+        copies = []
+        for hop in range(1, radix):
+            partner, theirs = partners[k][hop]
+            give = starts[g] + theirs * rows if shares else starts[g]
+            copy = pltpu.make_async_remote_copy(
+                src_ref=stats.at[:, rows_at(give, rows), :],
+                dst_ref=halves[k].at[g, hop - 1],
+                send_sem=rs_send.at[g, slots[k] + hop - 1],
+                recv_sem=rs_recv.at[g, slots[k] + hop - 1],
+                device_id={"gx": partner},
+                device_id_type=MESH,
+            )
+            copy.start()
+            copies.append(copy)
+        flying[g] = copies
+        if shares:
+            starts[g] = starts[g] + mine * rows
+
+    def reduce_end(g, k):
+        distance, radix, rows, shares = stages[k]
+        for copy in flying[g]:
+            copy.wait_recv()
+            if shares:
+                pending.append(copy)
+            else:
+                copy.wait_send()
+        at = rows_at(starts[g], rows)
+        held = [stats[:, at, :].astype(F32)]
+        held += [halves[k][g, hop].astype(F32) for hop in range(radix - 1)]
+        peak = functools.reduce(jnp.maximum, [each[0] for each in held])
+        scales = [jnp.exp(each[0] - peak) for each in held]
+        norm = sum(each[1] * scale for each, scale in zip(held, scales))
+        total = sum(each[2] * scale for each, scale in zip(held, scales))
+        if k + 1 < len(stages):
+            stats[:, at, :] = jnp.stack([peak, norm, total]).astype(BF16)
+        else:
+            pooled[rows_at(PAD + starts[g], rows), :] = (total / norm).astype(BF16)
+
+    def gather_copy(g, slot, start, rows, partner):
+        part = pooled.at[rows_at(PAD + start, rows), :]
+        copy = pltpu.make_async_remote_copy(
+            src_ref=part,
+            dst_ref=part,
+            send_sem=ag_send.at[g, slot],
+            recv_sem=ag_recv.at[g, slot],
+            device_id={"gx": partner},
             device_id_type=MESH,
         )
-
-    for side in range(2):
-        _, norm, total = running[side]
-        strip[1 + side] = (total / norm).astype(BF16).astype(F32)
+        copy.start()
+        pending.append(copy)
+        return copy
+
+    def gather_far(g):
+        rows = stages[-1][2]
+        flying[g] = [
+            gather_copy(g, i, starts[g], rows, partner) for i, partner in enumerate(far)
+        ]
+
+    def gather_near(g):
+        for copy in flying[g]:
+            copy.wait_recv()
+        rows = stages[0][2]
+        flying[g] = [
+            gather_copy(g, len(far), g * tile + digits[0] * rows, rows, partners[0][1][0])
+        ]
+
+    def gather_end(g):
+        for copy in flying[g]:
+            copy.wait_recv()
 
     def strip_copy(side):
         return pltpu.make_async_remote_copy(
@@ -308,85 +410,66 @@
             device_id_type=MESH,
         )
 
-    start = 0
-    pending = []
-    for k, (distance, rows, halved) in enumerate(stages):
-        if halved:
-            give, keep = start + (1 - bits[k]) * rows, start + bits[k] * rows
-        else:
-            give = keep = start
-        copy = reduce_copy(k, give)
-        copy.start()
-        pending.append(copy)
-        if k == 0:
-            for side, has in ((0, has_left), (1, has_right)):
-
-                @pl.when(has)
-                def _():
-                    strip_copy(side).start()
-
-        copy.wait_recv()
-        if not halved:
-            copy.wait_send()
-            pending.pop()
-        start = pl.multiple_of(keep, 16)
-        mine = stats[:, pl.ds(start, rows), :].astype(F32)
-        other = halves[k][...].astype(F32)
-        peak = jnp.maximum(mine[0], other[0])
-        up, down = jnp.exp(mine[0] - peak), jnp.exp(other[0] - peak)
-        norm = mine[1] * up + other[1] * down
-        total = mine[2] * up + other[2] * down
-        if k + 1 < len(stages):
-            stats[:, pl.ds(start, rows), :] = jnp.stack([peak, norm, total]).astype(BF16)
-        else:
-            pooled[pl.ds(pl.multiple_of(PAD + start, 16), rows), :] = (total / norm).astype(BF16)
-
-    for k, (distance, rows, halved) in reversed(list(enumerate(stages))):
-        if not halved:
-            continue
-        part = pooled.at[pl.ds(pl.multiple_of(PAD + start, 16), rows), :]
-        copy = pltpu.make_async_remote_copy(
-            src_ref=part,
-            dst_ref=part,
-            send_sem=ag_send.at[k],
-            recv_sem=ag_recv.at[k],
-            device_id={"gx": partners[k]},
-            device_id_type=MESH,
-        )
-        copy.start()
-        pending.append(copy)
-        copy.wait_recv()
-        start = start - bits[k] * rows
-
-    for side, has in ((0, has_left), (1, has_right)):
-
-        @pl.when(has)
-        def _():
-            strip_copy(1 - side).wait_recv()
-
-    rows_z = [shifted(strip[i], depth) for i in range(4)]
-    stacked = [
-        jnp.concatenate([part for i in range(3) for part in rows_z[x + i]], axis=1)
-        for x in range(2)
-    ]
-    plane_xz = dot(jnp.concatenate(stacked, axis=0).astype(BF16), w_xz[...])
-    plane_xz = plane_xz.astype(BF16).astype(F32)
-    gain = norm_gain[...]
-
-    def finish(t, _):
-        at = pl.ds(pl.multiple_of(t * tile, 16), tile)
+    def strip_start():
+        for side, has in ((0, has_left), (1, has_right)):
+            _, norm, total = running[side]
+            strip[1 + side] = (total / norm).astype(BF16).astype(F32)
+
+            @pl.when(has)
+            def _():
+                strip_copy(side).start()
+
+    def strip_plane():
+        for side, has in ((0, has_left), (1, has_right)):
+
+            @pl.when(has)
+            def _():
+                strip_copy(1 - side).wait_recv()
+
+        rows_z = [shifted(strip[i], depth) for i in range(4)]
+        stacked = [
+            jnp.concatenate([part for i in range(3) for part in rows_z[x + i]], axis=1)
+            for x in range(2)
+        ]
+        plane = dot(jnp.concatenate(stacked, axis=0).astype(BF16), w_xz[...])
+        return plane.astype(BF16).astype(F32)
+
+    def finish(t):
+        at = slice(t * tile, (t + 1) * tile)
         plane_yz = dot(neighbourhood(pooled, t * tile, tile, depth), w_yz[...])
         plane_yz = plane_yz.astype(BF16).astype(F32).reshape(cells, depth, channels)
         for side in range(2):
             mixing = plane_yz + plane_xz[side * depth : (side + 1) * depth][None]
             joined = feature[side, at, :].astype(F32) * mixing.reshape(tile, channels)
             scale = lax.rsqrt(jnp.mean(joined * joined, axis=-1, keepdims=True) + 1e-06)
-            normed = (joined * scale * gain).astype(BF16)
+            normed = (joined * scale * norm_gain[...]).astype(BF16)
             hidden = activate(dot(normed, w_in[...])).astype(BF16)
             out[side, at, :] = (joined + dot(hidden, w_out[...])).astype(BF16)
-        return 0
-
-    lax.fori_loop(0, tiles, finish, 0)
+
+    last = len(stages)
+    plane_xz = None
+    for slot in range(tiles + last + 3):
+        if slot < tiles:
+            local_part(slot)
+        if slot == tiles - 1:
+            strip_start()
+        for g in range(tiles):
+            step = slot - g
+            if 1 <= step <= last:
+                reduce_end(g, step - 1)
+            if 0 <= step < last:
+                reduce_start(g, step)
+            if step == last:
+                gather_far(g)
+            if step == last + 1:
+                gather_near(g)
+            if step == last + 2:
+                gather_end(g)
+        if slot == tiles:
+            plane_xz = strip_plane()
+        ready = slot - last - 3
+        if 0 <= ready < tiles:
+            finish(ready)
 
     for copy in pending:
         copy.wait_send()
@@ -419,7 +502,8 @@
     hidden = mlp_in.shape[1]
     tile = min(256, length)
     tiles = length // tile
-    stages = stages_of(length, n)
+    stages = stages_of(tile, n)
+    exchanges = sum(stage[1] - 1 for stage in stages)
     padded = length + 2 * PAD
     taps = conv_first.shape[0] // 3 * channels
     hbm = pl.BlockSpec(memory_space=pl.ANY)
@@ -446,24 +530,27 @@
             pltpu.VMEM((3, length, channels), BF16),
             pltpu.VMEM((padded, channels), BF16),
             pltpu.VMEM((4, depth, channels), F32),
-            [pltpu.VMEM((3, stage[1], channels), BF16) for stage in stages],
+            [
+                pltpu.VMEM((tiles, radix - 1, 3, share, channels), BF16)
+                for _, radix, share, _ in stages
+            ],
             pltpu.SemaphoreType.DMA((12,)),
             pltpu.SemaphoreType.DMA((2,)),
             pltpu.SemaphoreType.DMA((2, 2, tiles)),
             pltpu.SemaphoreType.DMA((2, 2, tiles)),
             pltpu.SemaphoreType.DMA((2,)),
             pltpu.SemaphoreType.DMA((2,)),
-            pltpu.SemaphoreType.DMA((len(stages),)),
-            pltpu.SemaphoreType.DMA((len(stages),)),
-            pltpu.SemaphoreType.DMA((len(stages),)),
-            pltpu.SemaphoreType.DMA((len(stages),)),
+            pltpu.SemaphoreType.DMA((tiles, exchanges)),
+            pltpu.SemaphoreType.DMA((tiles, exchanges)),
+            pltpu.SemaphoreType.DMA((tiles, far_radix(stages))),
+            pltpu.SemaphoreType.DMA((tiles, far_radix(stages))),
         ],
         compiler_params=pltpu.CompilerParams(
-            collective_id=0, has_side_effects=True, vmem_limit_bytes=48 * 1024 * 1024
+            collective_id=0, has_side_effects=True, vmem_limit_bytes=62 * 1024 * 1024
         ),
     )(
         voxels.reshape(rows, length, channels),
-        prior,
+        prior.transpose(0, 2, 1),
         conv_first.reshape(3, taps, channels),
         conv_second.reshape(3, taps, channels),
         score_x,

time: 60.3 us -> 53.2 us (0.88)
  the two profiles are of different devices: /device:TPU:17 before, /device:TPU:0 now
where the time goes in v2:
time: 53.2 us; the launch traced here: 53 us
  Pallas kernels  51.1 us (96%)
  local copies, waits for them, and re-layouts  1.87 us (4%)
    pallas_call x1, Pallas kernels, on_device(): pl.pallas_call(functools.partial(kernel, n, tile, stages), out_shape=jax....  51.1 us
    unnamed x1, local copies, waits for them, and re-layouts  1.87 us

profile of v2, /device:TPU:0, one launch (start us, length us, event | category | flops | bytes accessed | tf_op | source)
XLA Modules:
  0.0 53.0 jit_solution(17605760040347933868)
XLA Ops:
  0.0 51.1 %shard_map.109 = bf16[2,1024,128]{2,1,0:T(8,128)(2,1)} custom-call(bf16[2,1024,128]{2,1,0:T(8,128)(2,1)} %bitcast.11, f32[2,8,128]{2,1,0:T(8,128)} %bitcast.14, bf16[3,1152,128]{2,1,0:T(8,128)(2,1)} %bitcast.9, bf16[3,1152,128]{2,1,0:T(8,128)(2,1)} %bitcast.10, bf16[128,128]{1,0:T(8,128)(2,1)} %score_x.1, bf16[128,128]{1,0:T(8,128)(2,1)} %score_y.1, ...), custom_call_target="tpu_custom_call" | custom-call | tf_op jit(solution)/shard_map/pallas_call | solution.py:511
  51.2 1.9 %copy.13 = bf16[2,128,8,128]{3,2,1,0:T(8,128)(2,1)} copy(bf16[2,128,8,128]{3,2,1,0:T(8,128)(2,1)} %bitcast.8) | data formatting | bytes 1048576

commit v3 on v2

--- a/solution.py
+++ b/solution.py
@@ -38,23 +38,30 @@
     return total
 
 
-def shifted(values, depth):
-    rows = values.shape[0]
-    at_z = lax.broadcasted_iota(jnp.int32, values.shape, 0) % depth
-    below = jnp.where(at_z == 0, 0.0, pltpu.roll(values, 1, 0))
-    above = jnp.where(at_z == depth - 1, 0.0, pltpu.roll(values, rows - 1, 0))
+def shifted(values):
+    depth = values.shape[1]
+    at_z = lax.broadcasted_iota(jnp.int32, (1,) + values.shape[1:], 1)
+    below = jnp.where(at_z == 0, 0.0, pltpu.roll(values, 1, 1))
+    above = jnp.where(at_z == depth - 1, 0.0, pltpu.roll(values, depth - 1, 1))
     return below, values, above
 
 
-def neighbourhood(padded, start, tile, depth):
-    window = padded[pl.ds(pl.multiple_of(start, 16), tile + 2 * PAD), :].astype(F32)
-    parts = shifted(window, depth)
-    columns = []
-    for along in (-1, 0, 1):
-        first = PAD + along * depth
-        for part in parts:
-            columns.append(part[first : first + tile].astype(BF16))
-    return jnp.concatenate(columns, axis=1)
+def stack(source, even, odd, start, rows, depth):
+    channels = source.shape[1]
+    window = source[pl.ds(pl.multiple_of(start - PAD, 16), rows + PAD), :].astype(F32)
+    parts = shifted(window.reshape(-1, depth, channels))
+    at = pl.ds(pl.multiple_of(start, 16), rows)
+    for i, part in enumerate(parts):
+        part = part.reshape(rows + PAD, channels)
+        columns = slice(i * channels, (i + 1) * channels)
+        even[at, columns] = part[PAD:].astype(BF16)
+        odd[at, columns] = part[PAD - depth : rows + PAD - depth].astype(BF16)
+
+
+def neighbourhood(even, odd, start, tile):
+    first = pl.ds(pl.multiple_of(start, 16), tile)
+    after = pl.ds(pl.multiple_of(start + PAD, 16), tile)
+    return jnp.concatenate([odd[first, :], even[first, :], odd[after, :]], axis=1)
 
 
 def dot(a, b):
@@ -93,6 +100,10 @@
     stats,
     pooled,
     strip,
+    running,
+    plane_xz,
+    even,
+    odd,
     halves,
     load_sem,
     vox_sem,
@@ -235,63 +246,114 @@
             def _():
                 vox_copy(side, t).start()
 
-    def inner(source, weight):
-        def body(t, _):
-            start = t * tile
-            total = dot(neighbourhood(source.at[0], start, tile, depth), weight[:, channels:])
-            total += dot(
-                neighbourhood(source.at[1], start, tile, depth), weight[:, : 2 * channels]
-            )
-            acc[pl.ds(pl.multiple_of(start, 16), tile), :] = total
-            return 0
-
-        lax.fori_loop(0, tiles, body, 0)
-
-    def outer(face, make, weight, side, t):
-        has = (has_left, has_right)[side]
-        if isinstance(t, int) and t == 0:
-            arrive(make, side, 0, has)
-        if t + 1 < tiles:
-            arrive(make, side, t + 1, has)
-        start = t * tile
+    def stack_tile(layer, source, t):
+        stack(source, even.at[layer], odd.at[layer], PAD + t * tile, tile, depth)
+
+    def stack_end(layer, source):
+        stack(source, even.at[layer], odd.at[layer], PAD + length, PAD, depth)
+
+    def around(layer, t):
+        return neighbourhood(even.at[layer], odd.at[layer], PAD + t * tile, tile)
+
+    def tile_at(t, offset=0):
+        return pl.ds(pl.multiple_of(offset + t * tile, 16), tile)
+
+    def inner(base, weight, t):
+        total = dot(around(base, t), weight[:, channels:])
+        total += dot(around(base + 1, t), weight[:, : 2 * channels])
+        acc[tile_at(t), :] = total
+
+    def face_tile(base, face, make, t):
+        for side, has in ((0, has_left), (1, has_right)):
+            arrive(make, side, t, has)
+            stack_tile(base + 2 + side, face.at[side], t)
+
+    def outer(base, weight, side, t):
         low = 2 * channels * (1 - side)
-        return acc[start : start + tile, side * channels : (side + 1) * channels] + dot(
-            neighbourhood(face.at[side], start, tile, depth), weight[:, low : low + channels]
+        return acc[tile_at(t), side * channels : (side + 1) * channels] + dot(
+            around(base + 2 + side, t), weight[:, low : low + channels]
         )
+
+    def repeat(count, body):
+        def step(t, carry):
+            body(t)
+            return carry
+
+        lax.fori_loop(0, count, step, 0)
 
     for copy in vox_loads + loads[:3]:
         copy.wait()
-    inner(vox, w_first)
-    for t in range(tiles):
-        for side, has in ((0, has_left), (1, has_right)):
-            value = activate(outer(face_vox, vox_copy, w_first, side, t)).astype(BF16)
-            first[side, PAD + t * tile : PAD + (t + 1) * tile, :] = value
-
-            @pl.when(has)
-            def _():
-                first_copy(side, t).start()
+
+    @functools.partial(repeat, tiles + 1)
+    def _(t):
+        @pl.when(t < tiles)
+        def _():
+            for side in range(2):
+                stack_tile(side, vox.at[side], t)
+
+        @pl.when(t == tiles)
+        def _():
+            for side in range(2):
+                stack_end(side, vox.at[side])
+
+        @pl.when(t >= 1)
+        def _():
+            inner(0, w_first, t - 1)
 
     for copy in loads[3:]:
         copy.wait()
-    inner(first, w_second)
+
+    @functools.partial(repeat, tiles + 2)
+    def _(t):
+        @pl.when(t < tiles)
+        def _():
+            face_tile(0, face_vox, vox_copy, t)
+
+        @pl.when(t == tiles)
+        def _():
+            for side in range(2):
+                stack_end(2 + side, face_vox.at[side])
+
+        @pl.when(jnp.logical_and(t >= 1, t <= tiles))
+        def _():
+            u = t - 1
+            for side, has in ((0, has_left), (1, has_right)):
+                value = activate(outer(0, w_first, side, u)).astype(BF16)
+                first[side, tile_at(u, PAD), :] = value
+
+                @pl.when(has)
+                def _():
+                    first_copy(side, u).start()
+
+            for side in range(2):
+                stack_tile(4 + side, first.at[side], u)
+
+        @pl.when(t == tiles)
+        def _():
+            for side in range(2):
+                stack_end(4 + side, first.at[side])
+
+        @pl.when(t >= 2)
+        def _():
+            inner(4, w_second, t - 2)
 
     cells = tile // depth
     cube = (cells, depth, across)
-    lane = lax.broadcasted_iota(jnp.int32, cube, 2)
-    cell = lax.broadcasted_iota(jnp.int32, cube, 0)
-    running = [None, None]
+    running[:, 0] = jnp.full((2, depth, channels), -jnp.inf, F32)
+    running[:, 1:] = jnp.zeros((2, 2, depth, channels), F32)
 
     def local_part(t):
         logits, features = [], []
+        lane = lax.broadcasted_iota(jnp.int32, cube, 2)
+        cell = lax.broadcasted_iota(jnp.int32, cube, 0) + t * cells
         for side in range(2):
-            start = PAD + t * tile
-            value = outer(face_first, first_copy, w_second, side, t)
-            value += vox[side, start : start + tile, :].astype(F32)
+            value = outer(4, w_second, side, t)
+            value += vox[side, tile_at(t, PAD), :].astype(F32)
             value = value.astype(BF16)
-            feature[side, t * tile : (t + 1) * tile, :] = value
+            feature[side, tile_at(t), :] = value
             both = dot(value, w_score[...])
             field = jnp.broadcast_to(prior[side][None], cube)
-            field = jnp.where(lane == cell + t * cells, field, 0.0)
+            field = jnp.where(lane == cell, field, 0.0)
             field = jnp.sum(field, axis=2, keepdims=True)
             field = jnp.broadcast_to(field, (cells, depth, channels))
             value = value.astype(F32)
@@ -299,64 +361,57 @@
             features.append(value)
             logit_y = both[:, channels:].reshape(cells, depth, channels) + field
             value = value.reshape(cells, depth, channels)
-            peak = jnp.max(logit_y, axis=0)
-            if running[side] is None:
-                weight = jnp.exp(logit_y - peak[None])
-                running[side] = (peak, jnp.sum(weight, 0), jnp.sum(weight * value, 0))
-            else:
-                old, norm, total = running[side]
-                peak = jnp.maximum(peak, old)
-                weight = jnp.exp(logit_y - peak[None])
-                keep = jnp.exp(old - peak)
-                running[side] = (
-                    peak,
-                    norm * keep + jnp.sum(weight, 0),
-                    total * keep + jnp.sum(weight * value, 0),
-                )
+            old, norm, total = running[side, 0], running[side, 1], running[side, 2]
+            peak = jnp.maximum(jnp.max(logit_y, axis=0), old)
+            weight = jnp.exp(logit_y - peak[None])
+            keep = jnp.exp(old - peak)
+            running[side, 0] = peak
+            running[side, 1] = norm * keep + jnp.sum(weight, 0)
+            running[side, 2] = total * keep + jnp.sum(weight * value, 0)
         peak = jnp.maximum(logits[0], logits[1]).astype(BF16)
         weights = [jnp.exp(logit - peak.astype(F32)) for logit in logits]
-        at = slice(t * tile, (t + 1) * tile)
-        stats[0, at, :] = peak
-        stats[1, at, :] = (weights[0] + weights[1]).astype(BF16)
-        stats[2, at, :] = (weights[0] * features[0] + weights[1] * features[1]).astype(BF16)
+        stats[0, tile_at(t), :] = peak
+        stats[1, tile_at(t), :] = (weights[0] + weights[1]).astype(BF16)
+        stats[2, tile_at(t), :] = (weights[0] * features[0] + weights[1] * features[1]).astype(BF16)
 
     def rows_at(start, rows):
         return pl.ds(pl.multiple_of(start, 16), rows)
 
-    starts = [t * tile for t in range(tiles)]
-    pending = []
-    flying = {}
-
-    def reduce_start(g, k):
+    def start_of(g, k):
+        start = g * tile
+        for digit, (_, _, rows, shares) in zip(digits[:k], stages):
+            if shares:
+                start = start + digit * rows
+        return start
+
+    def reduce_copies(g, k):
         distance, radix, rows, shares = stages[k]
-        mine = digits[k]
         copies = []
         for hop in range(1, radix):
             partner, theirs = partners[k][hop]
-            give = starts[g] + theirs * rows if shares else starts[g]
-            copy = pltpu.make_async_remote_copy(
-                src_ref=stats.at[:, rows_at(give, rows), :],
-                dst_ref=halves[k].at[g, hop - 1],
-                send_sem=rs_send.at[g, slots[k] + hop - 1],
-                recv_sem=rs_recv.at[g, slots[k] + hop - 1],
-                device_id={"gx": partner},
-                device_id_type=MESH,
+            give = start_of(g, k)
+            if shares:
+                give = give + theirs * rows
+            copies.append(
+                pltpu.make_async_remote_copy(
+                    src_ref=stats.at[:, rows_at(give, rows), :],
+                    dst_ref=halves[k].at[g, hop - 1],
+                    send_sem=rs_send.at[g, slots[k] + hop - 1],
+                    recv_sem=rs_recv.at[g, slots[k] + hop - 1],
+                    device_id={"gx": partner},
+                    device_id_type=MESH,
+                )
             )
-            copy.start()
-            copies.append(copy)
-        flying[g] = copies
-        if shares:
-            starts[g] = starts[g] + mine * rows
+        return copies
 
     def reduce_end(g, k):
         distance, radix, rows, shares = stages[k]
-        for copy in flying[g]:
+        for copy in reduce_copies(g, k):
             copy.wait_recv()
-            if shares:
-                pending.append(copy)
-            else:
+            if not shares:
                 copy.wait_send()
-        at = rows_at(starts[g], rows)
+        start = start_of(g, k + 1)
+        at = rows_at(start, rows)
         held = [stats[:, at, :].astype(F32)]
         held += [halves[k][g, hop].astype(F32) for hop in range(radix - 1)]
         peak = functools.reduce(jnp.maximum, [each[0] for each in held])
@@ -364,13 +419,14 @@
         norm = sum(each[1] * scale for each, scale in zip(held, scales))
         total = sum(each[2] * scale for each, scale in zip(held, scales))
         if k + 1 < len(stages):
-            stats[:, at, :] = jnp.stack([peak, norm, total]).astype(BF16)
+            for i, value in enumerate((peak, norm, total)):
+                stats[i, at, :] = value.astype(BF16)
         else:
-            pooled[rows_at(PAD + starts[g], rows), :] = (total / norm).astype(BF16)
+            pooled[rows_at(PAD + start, rows), :] = (total / norm).astype(BF16)
 
     def gather_copy(g, slot, start, rows, partner):
         part = pooled.at[rows_at(PAD + start, rows), :]
-        copy = pltpu.make_async_remote_copy(
+        return pltpu.make_async_remote_copy(
             src_ref=part,
             dst_ref=part,
             send_sem=ag_send.at[g, slot],
@@ -378,27 +434,14 @@
             device_id={"gx": partner},
             device_id_type=MESH,
         )
-        copy.start()
-        pending.append(copy)
-        return copy
-
-    def gather_far(g):
-        rows = stages[-1][2]
-        flying[g] = [
-            gather_copy(g, i, starts[g], rows, partner) for i, partner in enumerate(far)
-        ]
-
-    def gather_near(g):
-        for copy in flying[g]:
-            copy.wait_recv()
+
+    def far_copies(g):
+        start, rows = start_of(g, len(stages)), stages[-1][2]
+        return [gather_copy(g, i, start, rows, partner) for i, partner in enumerate(far)]
+
+    def near_copies(g):
         rows = stages[0][2]
-        flying[g] = [
-            gather_copy(g, len(far), g * tile + digits[0] * rows, rows, partners[0][1][0])
-        ]
-
-    def gather_end(g):
-        for copy in flying[g]:
-            copy.wait_recv()
+        return [gather_copy(g, len(far), start_of(g, 1), rows, partners[0][1][0])]
 
     def strip_copy(side):
         return pltpu.make_async_remote_copy(
@@ -412,8 +455,7 @@
 
     def strip_start():
         for side, has in ((0, has_left), (1, has_right)):
-            _, norm, total = running[side]
-            strip[1 + side] = (total / norm).astype(BF16).astype(F32)
+            strip[1 + side] = (running[side, 2] / running[side, 1]).astype(BF16).astype(F32)
 
             @pl.when(has)
             def _():
@@ -426,53 +468,97 @@
             def _():
                 strip_copy(1 - side).wait_recv()
 
-        rows_z = [shifted(strip[i], depth) for i in range(4)]
+        moved = shifted(strip[...])
         stacked = [
-            jnp.concatenate([part for i in range(3) for part in rows_z[x + i]], axis=1)
+            jnp.concatenate([part[x + i] for i in range(3) for part in moved], axis=1)
             for x in range(2)
         ]
         plane = dot(jnp.concatenate(stacked, axis=0).astype(BF16), w_xz[...])
-        return plane.astype(BF16).astype(F32)
+        plane_xz[...] = plane.astype(BF16).astype(F32)
 
     def finish(t):
-        at = slice(t * tile, (t + 1) * tile)
-        plane_yz = dot(neighbourhood(pooled, t * tile, tile, depth), w_yz[...])
+        plane_yz = dot(around(8, t), w_yz[...])
         plane_yz = plane_yz.astype(BF16).astype(F32).reshape(cells, depth, channels)
         for side in range(2):
-            mixing = plane_yz + plane_xz[side * depth : (side + 1) * depth][None]
-            joined = feature[side, at, :].astype(F32) * mixing.reshape(tile, channels)
+            mixing = plane_yz + plane_xz[side * depth : (side + 1) * depth, :][None]
+            joined = feature[side, tile_at(t), :].astype(F32) * mixing.reshape(tile, channels)
             scale = lax.rsqrt(jnp.mean(joined * joined, axis=-1, keepdims=True) + 1e-06)
             normed = (joined * scale * norm_gain[...]).astype(BF16)
             hidden = activate(dot(normed, w_in[...])).astype(BF16)
-            out[side, at, :] = (joined + dot(hidden, w_out[...])).astype(BF16)
+            out[side, tile_at(t), :] = (joined + dot(hidden, w_out[...])).astype(BF16)
 
     last = len(stages)
-    plane_xz = None
-    for slot in range(tiles + last + 3):
-        if slot < tiles:
-            local_part(slot)
-        if slot == tiles - 1:
+
+    @functools.partial(repeat, tiles + last + 4)
+    def _(slot):
+        @pl.when(slot < tiles)
+        def _():
+            face_tile(4, face_first, first_copy, slot)
+
+        @pl.when(slot == tiles)
+        def _():
+            for side in range(2):
+                stack_end(6 + side, face_first.at[side])
+
+        @pl.when(jnp.logical_and(slot >= 1, slot <= tiles))
+        def _():
+            local_part(slot - 1)
+
+        def at_step(step, body):
+            g = slot - 1 - step
+
+            @pl.when(jnp.logical_and(g >= 0, g < tiles))
+            def _():
+                body(g)
+
+        def start_all(copies):
+            for copy in copies:
+                copy.start()
+
+        def end_all(copies):
+            for copy in copies:
+                copy.wait_recv()
+
+        def advance(k, g):
+            if k > 0:
+                reduce_end(g, k - 1)
+            start_all(reduce_copies(g, k) if k < last else far_copies(g))
+
+        def gather_near(g):
+            end_all(far_copies(g))
+            start_all(near_copies(g))
+
+        def gather_end(g):
+            end_all(near_copies(g))
+            stack_tile(8, pooled, g)
+
+            @pl.when(g == tiles - 1)
+            def _():
+                stack_end(8, pooled)
+
+        for k in range(last + 1):
+            at_step(k, functools.partial(advance, k))
+        at_step(last + 1, gather_near)
+        at_step(last + 2, gather_end)
+
+        @pl.when(slot == tiles)
+        def _():
             strip_start()
-        for g in range(tiles):
-            step = slot - g
-            if 1 <= step <= last:
-                reduce_end(g, step - 1)
-            if 0 <= step < last:
-                reduce_start(g, step)
-            if step == last:
-                gather_far(g)
-            if step == last + 1:
-                gather_near(g)
-            if step == last + 2:
-                gather_end(g)
-        if slot == tiles:
-            plane_xz = strip_plane()
-        ready = slot - last - 3
-        if 0 <= ready < tiles:
-            finish(ready)
-
-    for copy in pending:
-        copy.wait_send()
+
+        @pl.when(slot == tiles + 1)
+        def _():
+            strip_plane()
+
+        at_step(last + 3, finish)
+
+    @functools.partial(repeat, tiles)
+    def _(g):
+        for k, (_, _, _, shares) in enumerate(stages):
+            for copy in reduce_copies(g, k) if shares else []:
+                copy.wait_send()
+        for copy in far_copies(g) + near_copies(g):
+            copy.wait_send()
+
     sent(vox_copy)
     sent(first_copy)
     for side, has in ((0, has_left), (1, has_right)):
@@ -530,6 +616,10 @@
             pltpu.VMEM((3, length, channels), BF16),
             pltpu.VMEM((padded, channels), BF16),
             pltpu.VMEM((4, depth, channels), F32),
+            pltpu.VMEM((2, 3, depth, channels), F32),
+            pltpu.VMEM((2 * depth, channels), F32),
+            pltpu.VMEM((9, padded, 3 * channels), BF16),
+            pltpu.VMEM((9, padded, 3 * channels), BF16),
             [
                 pltpu.VMEM((tiles, radix - 1, 3, share, channels), BF16)
                 for _, radix, share, _ in stages

time: 53.2 us -> 48.9 us (0.919)
  Pallas kernels: 51.1 us -> 46.8 us
    pallas_call x1, Pallas kernels: 51.1 us -> 46.8 us  [on_device(): pl.pallas_call(functools.partial(kernel, n, tile, stages), out_shape=jax....]
where the time goes in v3:
time: 48.9 us; the launch traced here: 48.7 us
  Pallas kernels  46.8 us (96%)
  local copies, waits for them, and re-layouts  1.87 us (4%)
    pallas_call x1, Pallas kernels, on_device(): pl.pallas_call(functools.partial(kernel, n, tile, stages), out_shape=jax....  46.8 us
    unnamed x1, local copies, waits for them, and re-layouts  1.87 us

profile of v3, /device:TPU:0, one launch (start us, length us, event | category | flops | bytes accessed | tf_op | source)
XLA Modules:
  0.0 48.7 jit_solution(5936477731973169382)
XLA Ops:
  0.0 46.8 %shard_map.109 = bf16[2,1024,128]{2,1,0:T(8,128)(2,1)} custom-call(bf16[2,1024,128]{2,1,0:T(8,128)(2,1)} %bitcast.11, f32[2,8,128]{2,1,0:T(8,128)} %bitcast.14, bf16[3,1152,128]{2,1,0:T(8,128)(2,1)} %bitcast.9, bf16[3,1152,128]{2,1,0:T(8,128)(2,1)} %bitcast.10, bf16[128,128]{1,0:T(8,128)(2,1)} %score_x.1, bf16[128,128]{1,0:T(8,128)(2,1)} %score_y.1, ...), custom_call_target="tpu_custom_call" | custom-call | tf_op jit(solution)/shard_map/pallas_call | solution.py:597
  46.8 1.9 %copy.13 = bf16[2,128,8,128]{3,2,1,0:T(8,128)(2,1)} copy(bf16[2,128,8,128]{3,2,1,0:T(8,128)(2,1)} %bitcast.8) | data formatting | bytes 1048576

commit v4 on v3

--- a/solution.py
+++ b/solution.py
@@ -102,6 +102,7 @@
     strip,
     running,
     plane_xz,
+    spread,
     even,
     odd,
     halves,
@@ -144,13 +145,13 @@
     slots = [sum(stage[1] - 1 for stage in stages[:k]) for k in range(len(stages))]
     far = [across_bits(2, hop) for hop in range(1, far_radix(stages))]
 
-    loads = [
-        (conv_first.at[tap], w_first.at[:, pl.ds((2 - tap) * channels, channels)]) for tap in range(3)
-    ]
-    loads += [
-        (conv_second.at[tap], w_second.at[:, pl.ds((2 - tap) * channels, channels)])
-        for tap in range(3)
-    ]
+    taps = conv_first.shape[1]
+    loads = []
+    for source, target in ((conv_first, w_first), (conv_second, w_second)):
+        for layer in range(2):
+            for result in range(2):
+                block = (pl.ds(layer * taps, taps), pl.ds(result * channels, channels))
+                loads.append((source.at[1 + layer - result], target.at[block]))
     loads += [
         (score_x, w_score.at[:, pl.ds(0, channels)]),
         (score_y, w_score.at[:, pl.ds(channels, channels)]),
@@ -259,9 +260,8 @@
         return pl.ds(pl.multiple_of(offset + t * tile, 16), tile)
 
     def inner(base, weight, t):
-        total = dot(around(base, t), weight[:, channels:])
-        total += dot(around(base + 1, t), weight[:, : 2 * channels])
-        acc[tile_at(t), :] = total
+        both = jnp.concatenate([around(base, t), around(base + 1, t)], axis=1)
+        acc[tile_at(t), :] = dot(both, weight[...])
 
     def face_tile(base, face, make, t):
         for side, has in ((0, has_left), (1, has_right)):
@@ -269,9 +269,12 @@
             stack_tile(base + 2 + side, face.at[side], t)
 
     def outer(base, weight, side, t):
-        low = 2 * channels * (1 - side)
+        if side == 0:
+            part = weight[:taps, channels:]
+        else:
+            part = weight[taps:, :channels]
         return acc[tile_at(t), side * channels : (side + 1) * channels] + dot(
-            around(base + 2 + side, t), weight[:, low : low + channels]
+            around(base + 2 + side, t), part
         )
 
     def repeat(count, body):
@@ -281,7 +284,19 @@
 
         lax.fori_loop(0, count, step, 0)
 
-    for copy in vox_loads + loads[:3]:
+    cells = tile // depth
+    cube = (cells, depth, across)
+
+    def spread_tile(t):
+        lane = lax.broadcasted_iota(jnp.int32, cube, 2)
+        cell = lax.broadcasted_iota(jnp.int32, cube, 0) + t * cells
+        for side in range(2):
+            field = jnp.broadcast_to(prior[side][None], cube)
+            field = jnp.sum(jnp.where(lane == cell, field, 0.0), axis=2, keepdims=True)
+            field = jnp.broadcast_to(field, (cells, depth, channels))
+            spread[side, tile_at(t), :] = field.reshape(tile, channels)
+
+    for copy in vox_loads + loads[:4]:
         copy.wait()
 
     @functools.partial(repeat, tiles + 1)
@@ -298,9 +313,10 @@
 
         @pl.when(t >= 1)
         def _():
+            spread_tile(t - 1)
             inner(0, w_first, t - 1)
 
-    for copy in loads[3:]:
+    for copy in loads[4:]:
         copy.wait()
 
     @functools.partial(repeat, tiles + 2)
@@ -337,29 +353,22 @@
         def _():
             inner(4, w_second, t - 2)
 
-    cells = tile // depth
-    cube = (cells, depth, across)
     running[:, 0] = jnp.full((2, depth, channels), -jnp.inf, F32)
     running[:, 1:] = jnp.zeros((2, 2, depth, channels), F32)
 
     def local_part(t):
         logits, features = [], []
-        lane = lax.broadcasted_iota(jnp.int32, cube, 2)
-        cell = lax.broadcasted_iota(jnp.int32, cube, 0) + t * cells
         for side in range(2):
             value = outer(4, w_second, side, t)
             value += vox[side, tile_at(t, PAD), :].astype(F32)
             value = value.astype(BF16)
             feature[side, tile_at(t), :] = value
             both = dot(value, w_score[...])
-            field = jnp.broadcast_to(prior[side][None], cube)
-            field = jnp.where(lane == cell, field, 0.0)
-            field = jnp.sum(field, axis=2, keepdims=True)
-            field = jnp.broadcast_to(field, (cells, depth, channels))
+            field = spread[side, tile_at(t), :]
             value = value.astype(F32)
-            logits.append(both[:, :channels] + field.reshape(tile, channels))
+            logits.append(both[:, :channels] + field)
             features.append(value)
-            logit_y = both[:, channels:].reshape(cells, depth, channels) + field
+            logit_y = (both[:, channels:] + field).reshape(cells, depth, channels)
             value = value.reshape(cells, depth, channels)
             old, norm, total = running[side, 0], running[side, 1], running[side, 2]
             peak = jnp.maximum(jnp.max(logit_y, axis=0), old)
@@ -482,7 +491,8 @@
         for side in range(2):
             mixing = plane_yz + plane_xz[side * depth : (side + 1) * depth, :][None]
             joined = feature[side, tile_at(t), :].astype(F32) * mixing.reshape(tile, channels)
-            scale = lax.rsqrt(jnp.mean(joined * joined, axis=-1, keepdims=True) + 1e-06)
+            squares = dot((joined * joined).astype(BF16), jnp.ones((channels, channels), BF16))
+            scale = lax.rsqrt(squares * (1.0 / channels) + 1e-06)
             normed = (joined * scale * norm_gain[...]).astype(BF16)
             hidden = activate(dot(normed, w_in[...])).astype(BF16)
             out[side, tile_at(t), :] = (joined + dot(hidden, w_out[...])).astype(BF16)
@@ -600,8 +610,8 @@
         in_specs=[hbm, vmem, hbm, hbm, hbm, hbm, hbm, hbm, vmem, hbm, hbm],
         out_specs=vmem,
         scratch_shapes=[
-            pltpu.VMEM((taps, 3 * channels), BF16),
-            pltpu.VMEM((taps, 3 * channels), BF16),
+            pltpu.VMEM((2 * taps, 2 * channels), BF16),
+            pltpu.VMEM((2 * taps, 2 * channels), BF16),
             pltpu.VMEM((channels, 2 * channels), BF16),
             pltpu.VMEM((taps, channels), BF16),
             pltpu.VMEM((taps, channels), BF16),
@@ -618,13 +628,14 @@
             pltpu.VMEM((4, depth, channels), F32),
             pltpu.VMEM((2, 3, depth, channels), F32),
             pltpu.VMEM((2 * depth, channels), F32),
+            pltpu.VMEM((2, length, channels), F32),
             pltpu.VMEM((9, padded, 3 * channels), BF16),
             pltpu.VMEM((9, padded, 3 * channels), BF16),
             [
                 pltpu.VMEM((tiles, radix - 1, 3, share, channels), BF16)
                 for _, radix, share, _ in stages
             ],
-            pltpu.SemaphoreType.DMA((12,)),
+            pltpu.SemaphoreType.DMA((14,)),
             pltpu.SemaphoreType.DMA((2,)),
             pltpu.SemaphoreType.DMA((2, 2, tiles)),
             pltpu.SemaphoreType.DMA((2, 2, tiles)),

time: 48.9 us -> 49.5 us (1.012)
  Pallas kernels: 46.8 us -> 47.4 us
    pallas_call x1, Pallas kernels: 46.8 us -> 47.4 us  [on_device(): pl.pallas_call(functools.partial(kernel, n, tile, stages), out_shape=jax....]
where the time goes in v4:
time: 49.5 us; the launch traced here: 49.3 us
  Pallas kernels  47.4 us (96%)
  local copies, waits for them, and re-layouts  1.87 us (4%)
    pallas_call x1, Pallas kernels, on_device(): pl.pallas_call(functools.partial(kernel, n, tile, stages), out_shape=jax....  47.4 us
    unnamed x1, local copies, waits for them, and re-layouts  1.87 us

profile of v4, /device:TPU:0, one launch (start us, length us, event | category | flops | bytes accessed | tf_op | source)
XLA Modules:
  0.0 49.3 jit_solution(15273813873962134680)
XLA Ops:
  0.0 47.4 %shard_map.109 = bf16[2,1024,128]{2,1,0:T(8,128)(2,1)} custom-call(bf16[2,1024,128]{2,1,0:T(8,128)(2,1)} %bitcast.11, f32[2,8,128]{2,1,0:T(8,128)} %bitcast.14, bf16[3,1152,128]{2,1,0:T(8,128)(2,1)} %bitcast.9, bf16[3,1152,128]{2,1,0:T(8,128)(2,1)} %bitcast.10, bf16[128,128]{1,0:T(8,128)(2,1)} %score_x.1, bf16[128,128]{1,0:T(8,128)(2,1)} %score_y.1, ...), custom_call_target="tpu_custom_call" | custom-call | tf_op jit(solution)/shard_map/pallas_call | solution.py:607
  47.5 1.9 %copy.13 = bf16[2,128,8,128]{3,2,1,0:T(8,128)(2,1)} copy(bf16[2,128,8,128]{3,2,1,0:T(8,128)(2,1)} %bitcast.8) | data formatting | bytes 1048576

commit v5 on v4

--- a/solution.py
+++ b/solution.py
@@ -596,7 +596,7 @@
     assert rows == 2 and depth == 8 and n & (n - 1) == 0
     length = across * depth
     hidden = mlp_in.shape[1]
-    tile = min(256, length)
+    tile = min(512, length)
     tiles = length // tile
     stages = stages_of(tile, n)
     exchanges = sum(stage[1] - 1 for stage in stages)

time: 49.5 us -> 48.5 us (0.980); the launches traced: 49.3 us -> 47.7 us
  Pallas kernels: 47.4 us -> 45.8 us
    pallas_call x1, Pallas kernels: 47.4 us -> 45.8 us  [on_device(): pl.pallas_call(functools.partial(kernel, n, tile, stages), out_shape=jax....]
where the time goes in v5:
time: 48.5 us; the launch traced here: 47.7 us
  Pallas kernels  45.8 us (94%)
  local copies, waits for them, and re-layouts  1.87 us (4%)
    pallas_call x1, Pallas kernels, on_device(): pl.pallas_call(functools.partial(kernel, n, tile, stages), out_shape=jax....  45.8 us
    unnamed x1, local copies, waits for them, and re-layouts  1.87 us

profile of v5, /device:TPU:0, one launch (start us, length us, event | category | flops | bytes accessed | tf_op | source)
XLA Modules:
  0.0 47.7 jit_solution(5394332928935840469)
XLA Ops:
  0.0 45.8 %shard_map.109 = bf16[2,1024,128]{2,1,0:T(8,128)(2,1)} custom-call(bf16[2,1024,128]{2,1,0:T(8,128)(2,1)} %bitcast.11, f32[2,8,128]{2,1,0:T(8,128)} %bitcast.14, bf16[3,1152,128]{2,1,0:T(8,128)(2,1)} %bitcast.9, bf16[3,1152,128]{2,1,0:T(8,128)(2,1)} %bitcast.10, bf16[128,128]{1,0:T(8,128)(2,1)} %score_x.1, bf16[128,128]{1,0:T(8,128)(2,1)} %score_y.1, ...), custom_call_target="tpu_custom_call" | custom-call | tf_op jit(solution)/shard_map/pallas_call | solution.py:607
  45.8 1.9 %copy.13 = bf16[2,128,8,128]{3,2,1,0:T(8,128)(2,1)} copy(bf16[2,128,8,128]{3,2,1,0:T(8,128)(2,1)} %bitcast.8) | data formatting | bytes 1048576

commit v6 on v5

--- a/solution.py
+++ b/solution.py
@@ -19,8 +19,8 @@
 
 def stages_of(rows, devices):
     count = devices.bit_length() - 1
-    bits = [[i] for i in range(min(2, count))]
-    bits += [list(range(i, min(i + 2, count))) for i in range(2, count, 2)]
+    bits = [[i] for i in range(count)]
+    bits[1:4] = bits[2:4] + bits[1:2]
     stages = []
     for group in bits:
         radix = 1 << len(group)

time: 48.5 us -> 51.5 us (1.062)
  Pallas kernels: 45.8 us -> 48.8 us
    pallas_call x1, Pallas kernels: 45.8 us -> 48.8 us  [on_device(): pl.pallas_call(functools.partial(kernel, n, tile, stages), out_shape=jax....]
where the time goes in v6:
time: 51.5 us; the launch traced here: 50.7 us
  Pallas kernels  48.8 us (95%)
  local copies, waits for them, and re-layouts  1.87 us (4%)
    pallas_call x1, Pallas kernels, on_device(): pl.pallas_call(functools.partial(kernel, n, tile, stages), out_shape=jax....  48.8 us
    unnamed x1, local copies, waits for them, and re-layouts  1.87 us

profile of v6, /device:TPU:0, one launch (start us, length us, event | category | flops | bytes accessed | tf_op | source)
XLA Modules:
  0.0 50.7 jit_solution(13324051586404751482)
XLA Ops:
  0.0 48.8 %shard_map.109 = bf16[2,1024,128]{2,1,0:T(8,128)(2,1)} custom-call(bf16[2,1024,128]{2,1,0:T(8,128)(2,1)} %bitcast.11, f32[2,8,128]{2,1,0:T(8,128)} %bitcast.14, bf16[3,1152,128]{2,1,0:T(8,128)(2,1)} %bitcast.9, bf16[3,1152,128]{2,1,0:T(8,128)(2,1)} %bitcast.10, bf16[128,128]{1,0:T(8,128)(2,1)} %score_x.1, bf16[128,128]{1,0:T(8,128)(2,1)} %score_y.1, ...), custom_call_target="tpu_custom_call" | custom-call | tf_op jit(solution)/shard_map/pallas_call | solution.py:607
  48.8 1.9 %copy.13 = bf16[2,128,8,128]{3,2,1,0:T(8,128)(2,1)} copy(bf16[2,128,8,128]{3,2,1,0:T(8,128)(2,1)} %bitcast.8) | data formatting | bytes 1048576

commit v7 on v4

--- a/solution.py
+++ b/solution.py
@@ -19,8 +19,9 @@
 
 def stages_of(rows, devices):
     count = devices.bit_length() - 1
-    bits = [[i] for i in range(min(2, count))]
-    bits += [list(range(i, min(i + 2, count))) for i in range(2, count, 2)]
+    bits = [[0], list(range(1, min(4, count)))]
+    bits += [list(range(i, min(i + 2, count))) for i in range(4, count, 2)]
+    bits = [group for group in bits if group and group[-1] < count]
     stages = []
     for group in bits:
         radix = 1 << len(group)
@@ -33,7 +34,7 @@
 def far_radix(stages):
     total = 1
     for distance, radix, _, shares in stages:
-        if shares and distance > 1:
+        if shares:
             total *= radix
     return total
 
@@ -143,7 +144,7 @@
             found[hop] = (other, (other // distance) % radix)
         partners.append(found)
     slots = [sum(stage[1] - 1 for stage in stages[:k]) for k in range(len(stages))]
-    far = [across_bits(2, hop) for hop in range(1, far_radix(stages))]
+    far = [across_bits(1, hop) for hop in range(1, far_radix(stages))]
 
     taps = conv_first.shape[1]
     loads = []
@@ -178,7 +179,7 @@
         partner
         for stage, found in zip(stages, partners)
         for partner, _ in found.values()
-        if stage[0] == 1 or not stage[3]
+        if not stage[3]
     ]
     for partner in greeted:
         pl.semaphore_signal(barrier, inc=1, device_id={"gx": partner}, device_id_type=MESH)
@@ -448,10 +449,6 @@
         start, rows = start_of(g, len(stages)), stages[-1][2]
         return [gather_copy(g, i, start, rows, partner) for i, partner in enumerate(far)]
 
-    def near_copies(g):
-        rows = stages[0][2]
-        return [gather_copy(g, len(far), start_of(g, 1), rows, partners[0][1][0])]
-
     def strip_copy(side):
         return pltpu.make_async_remote_copy(
             src_ref=strip.at[1 + side],
@@ -499,7 +496,7 @@
 
     last = len(stages)
 
-    @functools.partial(repeat, tiles + last + 4)
+    @functools.partial(repeat, tiles + last + 3)
     def _(slot):
         @pl.when(slot < tiles)
         def _():
@@ -534,12 +531,8 @@
                 reduce_end(g, k - 1)
             start_all(reduce_copies(g, k) if k < last else far_copies(g))
 
-        def gather_near(g):
+        def gather_end(g):
             end_all(far_copies(g))
-            start_all(near_copies(g))
-
-        def gather_end(g):
-            end_all(near_copies(g))
             stack_tile(8, pooled, g)
 
             @pl.when(g == tiles - 1)
@@ -548,8 +541,7 @@
 
         for k in range(last + 1):
             at_step(k, functools.partial(advance, k))
-        at_step(last + 1, gather_near)
-        at_step(last + 2, gather_end)
+        at_step(last + 1, gather_end)
 
         @pl.when(slot == tiles)
         def _():
@@ -559,14 +551,14 @@
         def _():
             strip_plane()
 
-        at_step(last + 3, finish)
+        at_step(last + 2, finish)
 
     @functools.partial(repeat, tiles)
     def _(g):
         for k, (_, _, _, shares) in enumerate(stages):
             for copy in reduce_copies(g, k) if shares else []:
                 copy.wait_send()
-        for copy in far_copies(g) + near_copies(g):
+        for copy in far_copies(g):
             copy.wait_send()
 
     sent(vox_copy)

time: 49.5 us -> 49.3 us (level)
  no operation moved by 1% of the time
where the time goes in v7:
time: 49.3 us; the launch traced here: 49.1 us
  Pallas kernels  47.2 us (96%)
  local copies, waits for them, and re-layouts  1.87 us (4%)
    pallas_call x1, Pallas kernels, on_device(): pl.pallas_call(functools.partial(kernel, n, tile, stages), out_shape=jax....  47.2 us
    unnamed x1, local copies, waits for them, and re-layouts  1.87 us

profile of v7, /device:TPU:0, one launch (start us, length us, event | category | flops | bytes accessed | tf_op | source)
XLA Modules:
  0.0 49.1 jit_solution(15702220068785753516)
XLA Ops:
  0.0 47.2 %shard_map.109 = bf16[2,1024,128]{2,1,0:T(8,128)(2,1)} custom-call(bf16[2,1024,128]{2,1,0:T(8,128)(2,1)} %bitcast.11, f32[2,8,128]{2,1,0:T(8,128)} %bitcast.14, bf16[3,1152,128]{2,1,0:T(8,128)(2,1)} %bitcast.9, bf16[3,1152,128]{2,1,0:T(8,128)(2,1)} %bitcast.10, bf16[128,128]{1,0:T(8,128)(2,1)} %score_x.1, bf16[128,128]{1,0:T(8,128)(2,1)} %score_y.1, ...), custom_call_target="tpu_custom_call" | custom-call | tf_op jit(solution)/shard_map/pallas_call | solution.py:599
  47.2 1.9 %copy.13 = bf16[2,128,8,128]{3,2,1,0:T(8,128)(2,1)} copy(bf16[2,128,8,128]{3,2,1,0:T(8,128)(2,1)} %bitcast.8) | data formatting | bytes 1048576

commit v8 on v7

--- a/solution.py
+++ b/solution.py
@@ -87,6 +87,7 @@
     out,
     w_first,
     w_second,
+    w_face,
     w_score,
     w_yz,
     w_xz,
@@ -148,7 +149,17 @@
 
     taps = conv_first.shape[1]
     loads = []
-    for source, target in ((conv_first, w_first), (conv_second, w_second)):
+    wide, third = 2 * taps // 3, taps // 3
+
+    def paired(source, target):
+        return [
+            (source.at[pl.ds(0, wide)], target.at[:, pl.ds(0, channels)]),
+            (source.at[pl.ds(wide, third)], target.at[pl.ds(third, third), pl.ds(channels, channels)]),
+        ]
+
+    for i, (source, target) in enumerate(((conv_first, w_first), (conv_second, w_second))):
+        for side in range(2):
+            loads += paired(source.at[2 * side], w_face.at[i, side])
         for layer in range(2):
             for result in range(2):
                 block = (pl.ds(layer * taps, taps), pl.ds(result * channels, channels))
@@ -156,11 +167,11 @@
     loads += [
         (score_x, w_score.at[:, pl.ds(0, channels)]),
         (score_y, w_score.at[:, pl.ds(channels, channels)]),
-        (plane_yz_w, w_yz),
         (plane_xz_w, w_xz),
         (mlp_in, w_in),
         (mlp_out, w_out),
     ]
+    loads += paired(plane_yz_w, w_yz)
     vox_loads = [
         pltpu.make_async_copy(
             voxels.at[row], vox.at[row, pl.ds(PAD, length), :], vox_sem.at[row]
@@ -192,6 +203,8 @@
     def _():
         pl.semaphore_signal(barrier, inc=1, device_id={"gx": right}, device_id_type=MESH)
 
+    w_face[:, :, :third, channels:] = jnp.zeros((2, 2, third, channels), BF16)
+    w_yz[:third, channels:] = jnp.zeros((third, channels), BF16)
     edge = jnp.zeros((2, PAD, channels), BF16)
     for padded in (vox, face_vox, first, face_first):
         padded[:, 0:PAD, :] = edge
@@ -269,13 +282,15 @@
             arrive(make, side, t, has)
             stack_tile(base + 2 + side, face.at[side], t)
 
+    def one_layer(layer, weight, t):
+        at = pl.ds(pl.multiple_of(PAD + t * tile, 16), tile + PAD)
+        both = jnp.concatenate([odd[layer, at, :], even[layer, at, :]], axis=1)
+        total = dot(both, weight)
+        return total[:tile, :channels] + total[depth : tile + depth, channels:]
+
     def outer(base, weight, side, t):
-        if side == 0:
-            part = weight[:taps, channels:]
-        else:
-            part = weight[taps:, :channels]
-        return acc[tile_at(t), side * channels : (side + 1) * channels] + dot(
-            around(base + 2 + side, t), part
+        return acc[tile_at(t), side * channels : (side + 1) * channels] + one_layer(
+            base + 2 + side, weight[side], t
         )
 
     def repeat(count, body):
@@ -297,7 +312,7 @@
             field = jnp.broadcast_to(field, (cells, depth, channels))
             spread[side, tile_at(t), :] = field.reshape(tile, channels)
 
-    for copy in vox_loads + loads[:4]:
+    for copy in vox_loads + loads[:8]:
         copy.wait()
 
     @functools.partial(repeat, tiles + 1)
@@ -317,7 +332,7 @@
             spread_tile(t - 1)
             inner(0, w_first, t - 1)
 
-    for copy in loads[4:]:
+    for copy in loads[8:]:
         copy.wait()
 
     @functools.partial(repeat, tiles + 2)
@@ -335,7 +350,7 @@
         def _():
             u = t - 1
             for side, has in ((0, has_left), (1, has_right)):
-                value = activate(outer(0, w_first, side, u)).astype(BF16)
+                value = activate(outer(0, w_face.at[0], side, u)).astype(BF16)
                 first[side, tile_at(u, PAD), :] = value
 
                 @pl.when(has)
@@ -360,7 +375,7 @@
     def local_part(t):
         logits, features = [], []
         for side in range(2):
-            value = outer(4, w_second, side, t)
+            value = outer(4, w_face.at[1], side, t)
             value += vox[side, tile_at(t, PAD), :].astype(F32)
             value = value.astype(BF16)
             feature[side, tile_at(t), :] = value
@@ -483,7 +498,7 @@
         plane_xz[...] = plane.astype(BF16).astype(F32)
 
     def finish(t):
-        plane_yz = dot(around(8, t), w_yz[...])
+        plane_yz = one_layer(8, w_yz[...], t)
         plane_yz = plane_yz.astype(BF16).astype(F32).reshape(cells, depth, channels)
         for side in range(2):
             mixing = plane_yz + plane_xz[side * depth : (side + 1) * depth, :][None]
@@ -588,7 +603,7 @@
     assert rows == 2 and depth == 8 and n & (n - 1) == 0
     length = across * depth
     hidden = mlp_in.shape[1]
-    tile = min(256, length)
+    tile = min(512, length)
     tiles = length // tile
     stages = stages_of(tile, n)
     exchanges = sum(stage[1] - 1 for stage in stages)
@@ -604,8 +619,9 @@
         scratch_shapes=[
             pltpu.VMEM((2 * taps, 2 * channels), BF16),
             pltpu.VMEM((2 * taps, 2 * channels), BF16),
+            pltpu.VMEM((2, 2, 2 * taps // 3, 2 * channels), BF16),
             pltpu.VMEM((channels, 2 * channels), BF16),
-            pltpu.VMEM((taps, channels), BF16),
+            pltpu.VMEM((2 * taps // 3, 2 * channels), BF16),
             pltpu.VMEM((taps, channels), BF16),
             pltpu.VMEM((channels, hidden), BF16),
             pltpu.VMEM((hidden, channels), BF16),
@@ -627,7 +643,7 @@
                 pltpu.VMEM((tiles, radix - 1, 3, share, channels), BF16)
                 for _, radix, share, _ in stages
             ],
-            pltpu.SemaphoreType.DMA((14,)),
+            pltpu.SemaphoreType.DMA((23,)),
             pltpu.SemaphoreType.DMA((2,)),
             pltpu.SemaphoreType.DMA((2, 2, tiles)),
             pltpu.SemaphoreType.DMA((2, 2, tiles)),

time: 49.3 us -> 49.6 us (level)
  no operation moved by 1% of the time
where the time goes in v8:
time: 49.6 us; the launch traced here: 49.4 us
  Pallas kernels  47.5 us (96%)
  local copies, waits for them, and re-layouts  1.87 us (4%)
    pallas_call x1, Pallas kernels, on_device(): pl.pallas_call(functools.partial(kernel, n, tile, stages), out_shape=jax....  47.5 us
    unnamed x1, local copies, waits for them, and re-layouts  1.87 us

profile of v8, /device:TPU:0, one launch (start us, length us, event | category | flops | bytes accessed | tf_op | source)
XLA Modules:
  0.0 49.4 jit_solution(7369508912745797486)
XLA Ops:
  0.0 47.5 %shard_map.109 = bf16[2,1024,128]{2,1,0:T(8,128)(2,1)} custom-call(bf16[2,1024,128]{2,1,0:T(8,128)(2,1)} %bitcast.11, f32[2,8,128]{2,1,0:T(8,128)} %bitcast.14, bf16[3,1152,128]{2,1,0:T(8,128)(2,1)} %bitcast.9, bf16[3,1152,128]{2,1,0:T(8,128)(2,1)} %bitcast.10, bf16[128,128]{1,0:T(8,128)(2,1)} %score_x.1, bf16[128,128]{1,0:T(8,128)(2,1)} %score_y.1, ...), custom_call_target="tpu_custom_call" | custom-call | tf_op jit(solution)/shard_map/pallas_call | solution.py:614
  47.5 1.9 %copy.13 = bf16[2,128,8,128]{3,2,1,0:T(8,128)(2,1)} copy(bf16[2,128,8,128]{3,2,1,0:T(8,128)(2,1)} %bitcast.8) | data formatting | bytes 1048576

commit v9 on v5

--- a/solution.py
+++ b/solution.py
@@ -170,9 +170,6 @@
         pltpu.make_async_copy(source, target, load_sem.at[i])
         for i, (source, target) in enumerate(loads)
     ]
-    for copy in vox_loads + loads:
-        copy.start()
-
     barrier = pltpu.get_barrier_semaphore()
     greeted = far + [
         partner
@@ -191,6 +188,9 @@
     def _():
         pl.semaphore_signal(barrier, inc=1, device_id={"gx": right}, device_id_type=MESH)
 
+    for copy in vox_loads:
+        copy.start()
+
     edge = jnp.zeros((2, PAD, channels), BF16)
     for padded in (vox, face_vox, first, face_first):
         padded[:, 0:PAD, :] = edge
@@ -246,6 +246,9 @@
             @pl.when(has)
             def _():
                 vox_copy(side, t).start()
+
+    for copy in loads:
+        copy.start()
 
     def stack_tile(layer, source, t):
         stack(source, even.at[layer], odd.at[layer], PAD + t * tile, tile, depth)

time: 48.5 us -> 48.5 us (level)
  no operation moved by 1% of the time
where the time goes in v9:
time: 48.5 us; the launch traced here: 47.7 us
  Pallas kernels  45.8 us (94%)
  local copies, waits for them, and re-layouts  1.87 us (4%)
    pallas_call x1, Pallas kernels, on_device(): pl.pallas_call(functools.partial(kernel, n, tile, stages), out_shape=jax....  45.8 us
    unnamed x1, local copies, waits for them, and re-layouts  1.87 us

profile of v9, /device:TPU:0, one launch (start us, length us, event | category | flops | bytes accessed | tf_op | source)
XLA Modules:
  0.0 47.7 jit_solution(154643327577695266)
XLA Ops:
  0.0 45.8 %shard_map.109 = bf16[2,1024,128]{2,1,0:T(8,128)(2,1)} custom-call(bf16[2,1024,128]{2,1,0:T(8,128)(2,1)} %bitcast.11, f32[2,8,128]{2,1,0:T(8,128)} %bitcast.14, bf16[3,1152,128]{2,1,0:T(8,128)(2,1)} %bitcast.9, bf16[3,1152,128]{2,1,0:T(8,128)(2,1)} %bitcast.10, bf16[128,128]{1,0:T(8,128)(2,1)} %score_x.1, bf16[128,128]{1,0:T(8,128)(2,1)} %score_y.1, ...), custom_call_target="tpu_custom_call" | custom-call | tf_op jit(solution)/shard_map/pallas_call | solution.py:610
  45.8 1.9 %copy.13 = bf16[2,128,8,128]{3,2,1,0:T(8,128)(2,1)} copy(bf16[2,128,8,128]{3,2,1,0:T(8,128)(2,1)} %bitcast.8) | data formatting | bytes 1048576
